TPU v7x, 32 devices: a whole 2x2x4 slice. The times are simulated.
32 devices in a mesh: gx: 4 (over y, core), gy: 8 (over z, x).
Axes of the slice: x: 2, y: 2, z: 4, core: 2. Of those that a mesh axis runs over, the one named last changes fastest.
Arguments:
- right_sides: float32 [16, 4, 16, 1024], P(None, None, 'gx', 'gy'), may hold values from -12 to 12, as said below
- coefficients: float32 [27, 4, 16, 1024], P(None, None, 'gx', 'gy'), may hold values from -0.045 to 2, as said below
Outputs:
- basis_q: float32 [80, 4, 16, 1024], P(None, None, 'gx', 'gy')
- factor_r: float32 [80, 80], replicated
Inputs may be any that keep to these rules, and one draw needn't show every extreme that they name: `right_sides`: each entry is the product of a value of order one and a factor that grows from 1 to 3 along x. `coefficients`: the centre coefficient (index 13) lies in 1 to 2, the other 26 in -0.045 to 0.015.
All inputs are finite; a program needn't handle non-finite values.
Results may differ from a plain program's by a relative error of at most 0.0003.
Values sent between devices are 32-bit elements; how exact they have to be, the bound alone decides.
A program may use at most 64 MiB of HBM per device.

v0:
```python
import jax
import jax.numpy as jnp
from jax import lax
from jax.sharding import PartitionSpec as P

STEPS = 4


OFFSETS = tuple(
    (
        (plane_step, row_step, col_step)
        for plane_step in (-1, 0, 1)
        for row_step in (-1, 0, 1)
        for col_step in (-1, 0, 1)
    )
)
CENTER_SHIFT = 1.5
HALF_SPAN = 0.5


def padded_2(array, sides, width):
    for axis, dim in sides:
        devices, length = (lax.axis_size(axis), array.shape[dim])
        up = [(i, (i + 1) % devices) for i in range(devices)]
        down = [(j, i) for i, j in up]
        last = lax.slice_in_dim(array, length - width, length, axis=dim)
        leading = lax.slice_in_dim(array, 0, width, axis=dim)
        before = lax.ppermute(last, axis, up)
        after = lax.ppermute(leading, axis, down)
        array = jnp.concatenate([before, array, after], axis=dim)
    return array


def apply_operator(padded, coefficients):
    planes, rows, columns = (coefficients.shape[1], coefficients.shape[2], coefficients.shape[3])
    result = jnp.zeros((padded.shape[0], planes, rows, columns), jnp.float32)
    for number, (plane_step, row_step, col_step) in enumerate(OFFSETS):
        window = padded[
            :,
            1 + plane_step : 1 + plane_step + planes,
            1 + row_step : 1 + row_step + rows,
            1 + col_step : 1 + col_step + columns,
        ]
        result = result + coefficients[number][None] * window
    return result


def chebyshev_next(padded, coefficients, previous):
    center = padded[:, 1:-1, 1:-1, 1:-1]
    shifted = (apply_operator(padded, coefficients) - CENTER_SHIFT * center) / HALF_SPAN
    if previous is None:
        return shifted
    return 2.0 * shifted - previous


def trim_edges(ghosted, margin):
    extent = ghosted.shape[-1]
    places = jnp.arange(extent)
    column = lax.axis_index("gy")
    last_column = lax.axis_size("gy") - 1
    outside = (column == 0) & (places < margin) | (column == last_column) & (
        places >= extent - margin
    )
    inside = jnp.logical_not(outside).astype(ghosted.dtype)
    return ghosted * inside


def pad_planes(ghosted):
    return jnp.pad(ghosted, ((0, 0), (1, 1), (0, 0), (0, 0)))


def local(right_sides, coefficients):
    blocks = [right_sides]
    previous = None
    current = right_sides
    for step in range(STEPS):
        ghosted = padded_2(current, (("gx", 2), ("gy", 3)), 1)
        ghosted = trim_edges(ghosted, 1)
        following = chebyshev_next(pad_planes(ghosted), coefficients, previous)
        previous, current = (current, following)
        blocks.append(current)
    stacked = jnp.concatenate(blocks, axis=0)
    flat = stacked.reshape(stacked.shape[0], -1)
    local_gram = jnp.dot(flat, flat.T, precision=lax.Precision.HIGHEST)
    gram_sum = lax.psum(local_gram, ("gx", "gy"))
    total_cells = flat.shape[1] * lax.axis_size("gx") * lax.axis_size("gy")
    gram = gram_sum / jnp.float32(total_cells)
    factor_lower = jnp.linalg.cholesky(gram)
    identity = jnp.eye(flat.shape[0], dtype=jnp.float32)
    inverse = jax.scipy.linalg.solve_triangular(factor_lower, identity, lower=True)
    solved = jnp.dot(inverse, flat, precision=lax.Precision.HIGHEST)
    return (solved.reshape(stacked.shape), factor_lower.T)


def solution(mesh):
    placed = (P(None, None, "gx", "gy"), P(None, None, "gx", "gy"))
    return jax.shard_map(
        local,
        mesh=mesh,
        in_specs=placed,
        out_specs=(P(None, None, "gx", "gy"), P()),
        check_vma=False,
    )
```

profile of v0, /device:TPU:0, one launch (start us, length us, event | category | flops | bytes accessed | tf_op | source)
XLA Modules:
  0.0 130.5 jit_solution(13103037171329206752)
XLA Ops:
  0.6 1.1 fusion.203
  2.2 2.0 %collective-permute-start.1 = (f32[16,4,1,128]{3,0,2,1:T(8,128)S(1)}, f32[16,4,1,128]{3,0,2,1:T(8,128)S(1)}, u32[]{:S(2)}, u32[]{:S(2)}) collective-permute-start(f32[16,4,1,128]{3,0,2,1:T(8,128)S(1)} %copy.33), channel_id=1, source_target_pairs={{8,0},{16,8},{24,16},{0,24},{9,1},{17,9},{25,17},{1,25},{10,2},{18... | collective-permute-start | bytes 98312 | tf_op jit(solution)/shard_map/ppermute | solution.py:29
  4.3 1.5 %collective-permute-done = f32[16,4,1,128]{3,0,2,1:T(8,128)S(1)} collective-permute-done((f32[16,4,1,128]{3,0,2,1:T(8,128)S(1)}, f32[16,4,1,128]{3,0,2,1:T(8,128)S(1)}, u32[]{:S(2)}, u32[]{:S(2)}) %collective-permute-start) | collective-permute-done | bytes 32800 | tf_op jit(solution)/shard_map/ppermute | solution.py:28
  6.1 2.2 %collective-permute-start.2 = (f32[16,4,6,1]{3,0,2,1:T(8,128)S(1)}, f32[16,4,6,1]{3,0,2,1:T(8,128)S(1)}, u32[]{:S(2)}, u32[]{:S(2)}) collective-permute-start(f32[16,4,6,1]{3,0,2,1:T(8,128)S(1)} %get-tuple-element.45), channel_id=1, source_target_pairs={{0,1},{1,2},{2,3},{3,4},{4,5},{5,6},{6,7},{7,0},{8,9},{9,10},{10,1... | collective-permute-start | bytes 4616 | tf_op jit(solution)/shard_map/ppermute | solution.py:28
  8.3 3.1 %collective-permute-start.3 = (f32[16,4,6,1]{3,0,2,1:T(8,128)S(1)}, f32[16,4,6,1]{3,0,2,1:T(8,128)S(1)}, u32[]{:S(2)}, u32[]{:S(2)}) collective-permute-start(f32[16,4,6,1]{3,0,2,1:T(8,128)S(1)} %get-tuple-element.46), channel_id=1, source_target_pairs={{1,0},{2,1},{3,2},{4,3},{5,4},{6,5},{7,6},{0,7},{9,8},{10,9},{11,1... | collective-permute-start | bytes 4616 | tf_op jit(solution)/shard_map/ppermute | solution.py:29
  11.4 5.9 %collective-permute-done.2 = f32[16,4,6,1]{3,0,2,1:T(8,128)S(1)} collective-permute-done((f32[16,4,6,1]{3,0,2,1:T(8,128)S(1)}, f32[16,4,6,1]{3,0,2,1:T(8,128)S(1)}, u32[]{:S(2)}, u32[]{:S(2)}) %collective-permute-start.2) | collective-permute-done | bytes 1568 | tf_op jit(solution)/shard_map/ppermute | solution.py:28
  17.3 2.7 %collective-permute-done.3 = f32[16,4,6,1]{3,0,2,1:T(8,128)S(1)} collective-permute-done((f32[16,4,6,1]{3,0,2,1:T(8,128)S(1)}, f32[16,4,6,1]{3,0,2,1:T(8,128)S(1)}, u32[]{:S(2)}, u32[]{:S(2)}) %collective-permute-start.3) | collective-permute-done | bytes 1568 | tf_op jit(solution)/shard_map/ppermute | solution.py:29
  21.1 1.6 %collective-permute-start.5 = (f32[16,4,1,128]{3,0,2,1:T(8,128)S(1)}, f32[16,4,1,128]{3,0,2,1:T(8,128)S(1)}, u32[]{:S(2)}, u32[]{:S(2)}) collective-permute-start(f32[16,4,1,128]{3,0,2,1:T(8,128)S(1)} %get-tuple-element.52), channel_id=1, source_target_pairs={{8,0},{16,8},{24,16},{0,24},{9,1},{17,9},{25,17},{1,25},{10,2},{18... | collective-permute-start | bytes 98312 | tf_op jit(solution)/shard_map/ppermute | solution.py:29
  22.7 1.6 %collective-permute-done.4 = f32[16,4,1,128]{3,0,2,1:T(8,128)S(1)} collective-permute-done((f32[16,4,1,128]{3,0,2,1:T(8,128)S(1)}, f32[16,4,1,128]{3,0,2,1:T(8,128)S(1)}, u32[]{:S(2)}, u32[]{:S(2)}) %collective-permute-start.4) | collective-permute-done | bytes 32800 | tf_op jit(solution)/shard_map/ppermute | solution.py:28
  24.5 4.7 %collective-permute-start.7 = (f32[16,4,6,1]{3,0,2,1:T(8,128)S(1)}, f32[16,4,6,1]{3,0,2,1:T(8,128)S(1)}, u32[]{:S(2)}, u32[]{:S(2)}) collective-permute-start(f32[16,4,6,1]{3,0,2,1:T(8,128)S(1)} %get-tuple-element.44), channel_id=1, source_target_pairs={{1,0},{2,1},{3,2},{4,3},{5,4},{6,5},{7,6},{0,7},{9,8},{10,9},{11,1... | collective-permute-start | bytes 4616 | tf_op jit(solution)/shard_map/ppermute | solution.py:29
  29.2 5.6 %collective-permute-done.6 = f32[16,4,6,1]{3,0,2,1:T(8,128)S(1)} collective-permute-done((f32[16,4,6,1]{3,0,2,1:T(8,128)S(1)}, f32[16,4,6,1]{3,0,2,1:T(8,128)S(1)}, u32[]{:S(2)}, u32[]{:S(2)}) %collective-permute-start.6) | collective-permute-done | bytes 1568 | tf_op jit(solution)/shard_map/ppermute | solution.py:28
  34.7 2.1 %collective-permute-done.7 = f32[16,4,6,1]{3,0,2,1:T(8,128)S(1)} collective-permute-done((f32[16,4,6,1]{3,0,2,1:T(8,128)S(1)}, f32[16,4,6,1]{3,0,2,1:T(8,128)S(1)}, u32[]{:S(2)}, u32[]{:S(2)}) %collective-permute-start.7) | collective-permute-done | bytes 1568 | tf_op jit(solution)/shard_map/ppermute | solution.py:29
  37.1 0.7 constant_dynamic-update-slice_fusion.4
  37.9 1.6 %collective-permute-start.9 = (f32[16,4,1,128]{3,0,2,1:T(8,128)S(1)}, f32[16,4,1,128]{3,0,2,1:T(8,128)S(1)}, u32[]{:S(2)}, u32[]{:S(2)}) collective-permute-start(f32[16,4,1,128]{3,0,2,1:T(8,128)S(1)} %get-tuple-element.50), channel_id=1, source_target_pairs={{8,0},{16,8},{24,16},{0,24},{9,1},{17,9},{25,17},{1,25},{10,2},{18... | collective-permute-start | bytes 98312 | tf_op jit(solution)/shard_map/ppermute | solution.py:29
  39.6 1.6 %collective-permute-done.8 = f32[16,4,1,128]{3,0,2,1:T(8,128)S(1)} collective-permute-done((f32[16,4,1,128]{3,0,2,1:T(8,128)S(1)}, f32[16,4,1,128]{3,0,2,1:T(8,128)S(1)}, u32[]{:S(2)}, u32[]{:S(2)}) %collective-permute-start.8) | collective-permute-done | bytes 32800 | tf_op jit(solution)/shard_map/ppermute | solution.py:28
  41.4 4.7 %collective-permute-start.11 = (f32[16,4,6,1]{3,0,2,1:T(8,128)S(1)}, f32[16,4,6,1]{3,0,2,1:T(8,128)S(1)}, u32[]{:S(2)}, u32[]{:S(2)}) collective-permute-start(f32[16,4,6,1]{3,0,2,1:T(8,128)S(1)} %get-tuple-element.42), channel_id=1, source_target_pairs={{1,0},{2,1},{3,2},{4,3},{5,4},{6,5},{7,6},{0,7},{9,8},{10,9},{11,1... | collective-permute-start | bytes 4616 | tf_op jit(solution)/shard_map/ppermute | solution.py:29
  46.1 5.4 %collective-permute-done.10 = f32[16,4,6,1]{3,0,2,1:T(8,128)S(1)} collective-permute-done((f32[16,4,6,1]{3,0,2,1:T(8,128)S(1)}, f32[16,4,6,1]{3,0,2,1:T(8,128)S(1)}, u32[]{:S(2)}, u32[]{:S(2)}) %collective-permute-start.10) | collective-permute-done | bytes 1568 | tf_op jit(solution)/shard_map/ppermute | solution.py:28
  51.5 2.7 %collective-permute-done.11 = f32[16,4,6,1]{3,0,2,1:T(8,128)S(1)} collective-permute-done((f32[16,4,6,1]{3,0,2,1:T(8,128)S(1)}, f32[16,4,6,1]{3,0,2,1:T(8,128)S(1)}, u32[]{:S(2)}, u32[]{:S(2)}) %collective-permute-start.11) | collective-permute-done | bytes 1568 | tf_op jit(solution)/shard_map/ppermute | solution.py:29
  54.4 0.6 constant_dynamic-update-slice_fusion.3
  55.3 1.6 %collective-permute-start.13 = (f32[16,4,1,128]{3,0,2,1:T(8,128)S(1)}, f32[16,4,1,128]{3,0,2,1:T(8,128)S(1)}, u32[]{:S(2)}, u32[]{:S(2)}) collective-permute-start(f32[16,4,1,128]{3,0,2,1:T(8,128)S(1)} %get-tuple-element.48), channel_id=1, source_target_pairs={{8,0},{16,8},{24,16},{0,24},{9,1},{17,9},{25,17},{1,25},{10,2},{18... | collective-permute-start | bytes 98312 | tf_op jit(solution)/shard_map/ppermute | solution.py:29
  56.9 1.6 %collective-permute-done.12 = f32[16,4,1,128]{3,0,2,1:T(8,128)S(1)} collective-permute-done((f32[16,4,1,128]{3,0,2,1:T(8,128)S(1)}, f32[16,4,1,128]{3,0,2,1:T(8,128)S(1)}, u32[]{:S(2)}, u32[]{:S(2)}) %collective-permute-start.12) | collective-permute-done | bytes 32800 | tf_op jit(solution)/shard_map/ppermute | solution.py:28
  58.7 4.7 %collective-permute-start.15 = (f32[16,4,6,1]{3,0,2,1:T(8,128)S(1)}, f32[16,4,6,1]{3,0,2,1:T(8,128)S(1)}, u32[]{:S(2)}, u32[]{:S(2)}) collective-permute-start(f32[16,4,6,1]{3,0,2,1:T(8,128)S(1)} %get-tuple-element.40), channel_id=1, source_target_pairs={{1,0},{2,1},{3,2},{4,3},{5,4},{6,5},{7,6},{0,7},{9,8},{10,9},{11,1... | collective-permute-start | bytes 4616 | tf_op jit(solution)/shard_map/ppermute | solution.py:29
  63.4 5.4 %collective-permute-done.14 = f32[16,4,6,1]{3,0,2,1:T(8,128)S(1)} collective-permute-done((f32[16,4,6,1]{3,0,2,1:T(8,128)S(1)}, f32[16,4,6,1]{3,0,2,1:T(8,128)S(1)}, u32[]{:S(2)}, u32[]{:S(2)}) %collective-permute-start.14) | collective-permute-done | bytes 1568 | tf_op jit(solution)/shard_map/ppermute | solution.py:28
  68.8 2.8 %collective-permute-done.15 = f32[16,4,6,1]{3,0,2,1:T(8,128)S(1)} collective-permute-done((f32[16,4,6,1]{3,0,2,1:T(8,128)S(1)}, f32[16,4,6,1]{3,0,2,1:T(8,128)S(1)}, u32[]{:S(2)}, u32[]{:S(2)}) %collective-permute-start.15) | collective-permute-done | bytes 1568 | tf_op jit(solution)/shard_map/ppermute | solution.py:29
  72.4 0.7 convolution_bitcast_fusion.1
  73.3 38.7 %psum.7 = f32[80,80]{0,1:T(8,128)S(1)} all-reduce(f32[80,80]{0,1:T(8,128)S(1)} %convolution_bitcast_fusion.1), channel_id=1, replica_groups=mesh['gx'=4,'gy'=8] {'gx','gy'}, use_global_device_ids=true, to_apply=%region_0.1 | all-reduce | flops 6400 | bytes 51200 | tf_op jit(solution)/shard_map/psum | solution.py:85
  112.8 7.3 %cholesky.17 = f32[80,80]{1,0:T(8,128)S(1)} custom-call(f32[80,80]{1,0:T(8,128)S(1)} %fusion.191), custom_call_target="Cholesky" | custom-call | tf_op jit(solution)/shard_map/jit(cholesky)/cholesky | solution.py:88
  120.8 0.7 fusion.192
  121.5 0.7 copy.23
  122.2 6.1 %custom-call.7 = f32[1,80,80]{1,2,0:T(8,128)S(1)} custom-call(f32[1,80,80]{2,1,0:T(8,128)S(1)} %get-tuple-element.58), custom_call_target="InvertDiagBlocksLowerTriangular" | custom-call | tf_op jit(solution)/shard_map/jit(_solve_triangular)/triangular_solve | solution.py:90
  128.6 0.9 fusion
  129.4 1.1 copy.22
  (48 shorter events, 6.0 us)
Async XLA Ops:
  0.6 3.6 %copy-start.1 = (f32[27,4,4,128]{3,2,1,0:T(4,128)S(1)}, f32[27,4,4,128]{3,2,1,0:T(4,128)}, u32[]{:S(2)}) copy-start(f32[27,4,4,128]{3,2,1,0:T(4,128)} %param.3) | copy-start | bytes 663556
  1.7 4.1 %collective-permute-start = (f32[16,4,1,128]{3,0,2,1:T(8,128)S(1)}, f32[16,4,1,128]{3,0,2,1:T(8,128)S(1)}, u32[]{:S(2)}, u32[]{:S(2)}) collective-permute-start(f32[16,4,1,128]{3,0,2,1:T(8,128)S(1)} %copy.32), channel_id=1, source_target_pairs={{0,8},{8,16},{16,24},{24,0},{1,9},{9,17},{17,25},{25,1},{2,10},{10... | collective-permute-start | bytes 98312 | tf_op jit(solution)/shard_map/ppermute | solution.py:28
  2.2 3.7 %collective-permute-start.1 = (f32[16,4,1,128]{3,0,2,1:T(8,128)S(1)}, f32[16,4,1,128]{3,0,2,1:T(8,128)S(1)}, u32[]{:S(2)}, u32[]{:S(2)}) collective-permute-start(f32[16,4,1,128]{3,0,2,1:T(8,128)S(1)} %copy.33), channel_id=1, source_target_pairs={{8,0},{16,8},{24,16},{0,24},{9,1},{17,9},{25,17},{1,25},{10,2},{18... | collective-permute-start | bytes 98312 | tf_op jit(solution)/shard_map/ppermute | solution.py:29
  4.3 1.5 %copy-start = (f32[16,4,4,128]{3,2,1,0:T(4,128)S(1)}, f32[16,4,4,128]{3,2,1,0:T(4,128)}, u32[]{:S(2)}) copy-start(f32[16,4,4,128]{3,2,1,0:T(4,128)} %param.2) | copy-start | bytes 393220
  6.1 11.2 %collective-permute-start.2 = (f32[16,4,6,1]{3,0,2,1:T(8,128)S(1)}, f32[16,4,6,1]{3,0,2,1:T(8,128)S(1)}, u32[]{:S(2)}, u32[]{:S(2)}) collective-permute-start(f32[16,4,6,1]{3,0,2,1:T(8,128)S(1)} %get-tuple-element.45), channel_id=1, source_target_pairs={{0,1},{1,2},{2,3},{3,4},{4,5},{5,6},{6,7},{7,0},{8,9},{9,10},{10,1... | collective-permute-start | bytes 4616 | tf_op jit(solution)/shard_map/ppermute | solution.py:28
  8.3 11.7 %collective-permute-start.3 = (f32[16,4,6,1]{3,0,2,1:T(8,128)S(1)}, f32[16,4,6,1]{3,0,2,1:T(8,128)S(1)}, u32[]{:S(2)}, u32[]{:S(2)}) collective-permute-start(f32[16,4,6,1]{3,0,2,1:T(8,128)S(1)} %get-tuple-element.46), channel_id=1, source_target_pairs={{1,0},{2,1},{3,2},{4,3},{5,4},{6,5},{7,6},{0,7},{9,8},{10,9},{11,1... | collective-permute-start | bytes 4616 | tf_op jit(solution)/shard_map/ppermute | solution.py:29
  20.9 3.4 %collective-permute-start.4 = (f32[16,4,1,128]{3,0,2,1:T(8,128)S(1)}, f32[16,4,1,128]{3,0,2,1:T(8,128)S(1)}, u32[]{:S(2)}, u32[]{:S(2)}) collective-permute-start(f32[16,4,1,128]{3,0,2,1:T(8,128)S(1)} %get-tuple-element.51), channel_id=1, source_target_pairs={{0,8},{8,16},{16,24},{24,0},{1,9},{9,17},{17,25},{25,1},{2,10},{10... | collective-permute-start | bytes 98312 | tf_op jit(solution)/shard_map/ppermute | solution.py:28
  21.1 3.2 %collective-permute-start.5 = (f32[16,4,1,128]{3,0,2,1:T(8,128)S(1)}, f32[16,4,1,128]{3,0,2,1:T(8,128)S(1)}, u32[]{:S(2)}, u32[]{:S(2)}) collective-permute-start(f32[16,4,1,128]{3,0,2,1:T(8,128)S(1)} %get-tuple-element.52), channel_id=1, source_target_pairs={{8,0},{16,8},{24,16},{0,24},{9,1},{17,9},{25,17},{1,25},{10,2},{18... | collective-permute-start | bytes 98312 | tf_op jit(solution)/shard_map/ppermute | solution.py:29
  24.4 10.3 %collective-permute-start.6 = (f32[16,4,6,1]{3,0,2,1:T(8,128)S(1)}, f32[16,4,6,1]{3,0,2,1:T(8,128)S(1)}, u32[]{:S(2)}, u32[]{:S(2)}) collective-permute-start(f32[16,4,6,1]{3,0,2,1:T(8,128)S(1)} %get-tuple-element.43), channel_id=1, source_target_pairs={{0,1},{1,2},{2,3},{3,4},{4,5},{5,6},{6,7},{7,0},{8,9},{9,10},{10,1... | collective-permute-start | bytes 4616 | tf_op jit(solution)/shard_map/ppermute | solution.py:28
  24.5 12.4 %collective-permute-start.7 = (f32[16,4,6,1]{3,0,2,1:T(8,128)S(1)}, f32[16,4,6,1]{3,0,2,1:T(8,128)S(1)}, u32[]{:S(2)}, u32[]{:S(2)}) collective-permute-start(f32[16,4,6,1]{3,0,2,1:T(8,128)S(1)} %get-tuple-element.44), channel_id=1, source_target_pairs={{1,0},{2,1},{3,2},{4,3},{5,4},{6,5},{7,6},{0,7},{9,8},{10,9},{11,1... | collective-permute-start | bytes 4616 | tf_op jit(solution)/shard_map/ppermute | solution.py:29
  37.8 3.4 %collective-permute-start.8 = (f32[16,4,1,128]{3,0,2,1:T(8,128)S(1)}, f32[16,4,1,128]{3,0,2,1:T(8,128)S(1)}, u32[]{:S(2)}, u32[]{:S(2)}) collective-permute-start(f32[16,4,1,128]{3,0,2,1:T(8,128)S(1)} %get-tuple-element.49), channel_id=1, source_target_pairs={{0,8},{8,16},{16,24},{24,0},{1,9},{9,17},{17,25},{25,1},{2,10},{10... | collective-permute-start | bytes 98312 | tf_op jit(solution)/shard_map/ppermute | solution.py:28
  37.9 3.2 %collective-permute-start.9 = (f32[16,4,1,128]{3,0,2,1:T(8,128)S(1)}, f32[16,4,1,128]{3,0,2,1:T(8,128)S(1)}, u32[]{:S(2)}, u32[]{:S(2)}) collective-permute-start(f32[16,4,1,128]{3,0,2,1:T(8,128)S(1)} %get-tuple-element.50), channel_id=1, source_target_pairs={{8,0},{16,8},{24,16},{0,24},{9,1},{17,9},{25,17},{1,25},{10,2},{18... | collective-permute-start | bytes 98312 | tf_op jit(solution)/shard_map/ppermute | solution.py:29
  41.3 10.2 %collective-permute-start.10 = (f32[16,4,6,1]{3,0,2,1:T(8,128)S(1)}, f32[16,4,6,1]{3,0,2,1:T(8,128)S(1)}, u32[]{:S(2)}, u32[]{:S(2)}) collective-permute-start(f32[16,4,6,1]{3,0,2,1:T(8,128)S(1)} %get-tuple-element.41), channel_id=1, source_target_pairs={{0,1},{1,2},{2,3},{3,4},{4,5},{5,6},{6,7},{7,0},{8,9},{9,10},{10,1... | collective-permute-start | bytes 4616 | tf_op jit(solution)/shard_map/ppermute | solution.py:28
  41.4 12.8 %collective-permute-start.11 = (f32[16,4,6,1]{3,0,2,1:T(8,128)S(1)}, f32[16,4,6,1]{3,0,2,1:T(8,128)S(1)}, u32[]{:S(2)}, u32[]{:S(2)}) collective-permute-start(f32[16,4,6,1]{3,0,2,1:T(8,128)S(1)} %get-tuple-element.42), channel_id=1, source_target_pairs={{1,0},{2,1},{3,2},{4,3},{5,4},{6,5},{7,6},{0,7},{9,8},{10,9},{11,1... | collective-permute-start | bytes 4616 | tf_op jit(solution)/shard_map/ppermute | solution.py:29
  55.1 3.4 %collective-permute-start.12 = (f32[16,4,1,128]{3,0,2,1:T(8,128)S(1)}, f32[16,4,1,128]{3,0,2,1:T(8,128)S(1)}, u32[]{:S(2)}, u32[]{:S(2)}) collective-permute-start(f32[16,4,1,128]{3,0,2,1:T(8,128)S(1)} %get-tuple-element.47), channel_id=1, source_target_pairs={{0,8},{8,16},{16,24},{24,0},{1,9},{9,17},{17,25},{25,1},{2,10},{10... | collective-permute-start | bytes 98312 | tf_op jit(solution)/shard_map/ppermute | solution.py:28
  55.3 3.2 %collective-permute-start.13 = (f32[16,4,1,128]{3,0,2,1:T(8,128)S(1)}, f32[16,4,1,128]{3,0,2,1:T(8,128)S(1)}, u32[]{:S(2)}, u32[]{:S(2)}) collective-permute-start(f32[16,4,1,128]{3,0,2,1:T(8,128)S(1)} %get-tuple-element.48), channel_id=1, source_target_pairs={{8,0},{16,8},{24,16},{0,24},{9,1},{17,9},{25,17},{1,25},{10,2},{18... | collective-permute-start | bytes 98312 | tf_op jit(solution)/shard_map/ppermute | solution.py:29
  58.6 10.1 %collective-permute-start.14 = (f32[16,4,6,1]{3,0,2,1:T(8,128)S(1)}, f32[16,4,6,1]{3,0,2,1:T(8,128)S(1)}, u32[]{:S(2)}, u32[]{:S(2)}) collective-permute-start(f32[16,4,6,1]{3,0,2,1:T(8,128)S(1)} %get-tuple-element.39), channel_id=1, source_target_pairs={{0,1},{1,2},{2,3},{3,4},{4,5},{5,6},{6,7},{7,0},{8,9},{9,10},{10,1... | collective-permute-start | bytes 4616 | tf_op jit(solution)/shard_map/ppermute | solution.py:28
  58.7 12.8 %collective-permute-start.15 = (f32[16,4,6,1]{3,0,2,1:T(8,128)S(1)}, f32[16,4,6,1]{3,0,2,1:T(8,128)S(1)}, u32[]{:S(2)}, u32[]{:S(2)}) collective-permute-start(f32[16,4,6,1]{3,0,2,1:T(8,128)S(1)} %get-tuple-element.40), channel_id=1, source_target_pairs={{1,0},{2,1},{3,2},{4,3},{5,4},{6,5},{7,6},{0,7},{9,8},{10,9},{11,1... | collective-permute-start | bytes 4616 | tf_op jit(solution)/shard_map/ppermute | solution.py:29
where the time goes:
time: 131 us
  waiting for transfers between devices  38.9 us (30%)
  blocking collectives  38.7 us (30%)
  starting transfers between devices  27.6 us (21%)
  other arithmetic  18.3 us (14%)
  local copies, waits for them, and re-layouts  4.45 us (3%)
  matrix products  1.75 us (1%)
    psum x1, blocking collectives, local(): gram_sum = lax.psum(local_gram, ('gx', 'gy'))  38.7 us
    ppermute x8, waiting for transfers between devices, padded_2(): before = lax.ppermute(last, axis, up)  28.5 us
    ppermute x8, starting transfers between devices, padded_2(): after = lax.ppermute(leading, axis, down)  24.1 us
    ppermute x8, waiting for transfers between devices, padded_2(): after = lax.ppermute(leading, axis, down)  10.4 us
    another operation x3, other arithmetic, local(): factor_lower = jnp.linalg.cholesky(gram)  7.98 us
    another operation x1, other arithmetic, local(): jax.scipy.linalg.solve_triangular(factor_lower, identity, lower=True)  6.13 us
    ppermute x8, starting transfers between devices, padded_2(): before = lax.ppermute(last, axis, up)  3.44 us
  transfers between devices with their start and end apart: 16, of which 13 were waited for; matrix products, arithmetic and copies ran while one was open for 0% of the time, Pallas kernels for 0%

commit v1 on v0

v1 whole, which is shorter than its diff:
```python
import functools

import jax
import jax.numpy as jnp
from jax import lax
from jax.experimental import pallas as pl
from jax.experimental.pallas import tpu as pltpu
from jax.sharding import PartitionSpec as P

MESH = pl.DeviceIdType.MESH
STEPS = 4
BLOCKS = STEPS + 1
LANES = 128
SIDES = (0, 1)
NT = (((1,), (1,)), ((), ()))
NN = (((1,), (0,)), ((), ()))


def dot(a, b, dims):
    return lax.dot_general(
        a, b, dims, precision=lax.Precision.HIGHEST, preferred_element_type=jnp.float32
    )


def each(start, stop, body):
    if stop - start <= 8:
        for i in range(start, stop):
            body(i)
    else:
        lax.fori_loop(start, stop, lambda i, c: (body(i), c)[1], 0)


def factor(square, rhs):
    row = lax.broadcasted_iota(jnp.int32, (rhs, LANES), 0)
    lane = lax.broadcasted_iota(jnp.int32, (rhs, LANES), 1)
    work = jnp.where(lane < rhs, square, jnp.where(lane - rhs == row, 1.0, 0.0))
    lower = jnp.zeros((rhs, LANES), jnp.float32)
    scale = jnp.zeros((rhs, LANES), jnp.float32)
    for k in range(rhs):
        column = jnp.broadcast_to(work[:, k : k + 1], (rhs, LANES))
        pivot_row = jnp.broadcast_to(work[k : k + 1, :], (rhs, LANES))
        pivot = jnp.broadcast_to(column[k : k + 1, :], (rhs, LANES))
        root = 1.0 / jnp.sqrt(pivot)
        lower = jnp.where((lane == k) & (row >= k), column * root, lower)
        scale = jnp.where(row == k, root, scale)
        work = work - jnp.where(row > k, column * (1.0 / pivot), 0.0) * pivot_row
    inverse = pltpu.roll(work * scale, LANES - rhs, 1)
    return lower, jnp.where(lane <= row, inverse, 0.0)


def kernel(
    nx, ny, rhs, nz, rows, total_cells,
    v_hbm, c_hbm, q_hbm, l_ref,
    v_in, c_in, wide, basis, tile, ghost, packed, landed, shifted, gram_x, gram_y,
    lower_inv, out,
    load_sem, store_sem, halo_send, halo_recv, gx_send, gx_recv, gy_send, gy_recv,
):
    gx, gy = lax.axis_index("gx"), lax.axis_index("gy")
    cells = nz * rows
    up, down = lax.rem(gx + 1, nx), lax.rem(gx + nx - 1, nx)
    has_left, has_right = gy > 0, gy < ny - 1
    around = (down, gx, up)
    there = (gy - 1, gy + 1)
    present = (has_left, has_right)

    load_v = pltpu.make_async_copy(v_hbm, v_in, load_sem.at[0])
    load_c = pltpu.make_async_copy(c_hbm, c_in, load_sem.at[1])
    load_v.start()
    load_c.start()

    barrier = pltpu.get_barrier_semaphore()

    def greet(x, y):
        pl.semaphore_signal(barrier, inc=1, device_id={"gx": x, "gy": y}, device_id_type=MESH)

    each(1, nx, lambda i: greet(lax.rem(gx + i, nx), gy))
    each(1, ny, lambda i: greet(gx, lax.rem(gy + i, ny)))
    for side in SIDES:
        @pl.when(present[side])
        def _():
            greet(down, there[side])
            greet(up, there[side])
    corners = 2 * has_left.astype(jnp.int32) + 2 * has_right.astype(jnp.int32)
    pl.semaphore_wait(barrier, (nx - 1) + (ny - 1) + corners)

    lane = lax.broadcasted_iota(jnp.int32, (rhs, LANES), 1)

    for side in SIDES:
        @pl.when(jnp.logical_not(present[side]))
        def _():
            for s in range(STEPS):
                landed[s, side] = jnp.zeros((3, rhs, LANES), jnp.float32)

    lower_inv[...] = jnp.zeros_like(lower_inv)

    def row_copy(s, side):
        return pltpu.make_async_remote_copy(
            src_ref=tile.at[s, :, rows - 1 if side == 0 else 0],
            dst_ref=ghost.at[s, side],
            send_sem=halo_send.at[s, side],
            recv_sem=halo_recv.at[s, side],
            device_id={"gx": up if side == 0 else down, "gy": gy},
            device_id_type=MESH,
        )

    def column_copy(s, side, slot):
        return pltpu.make_async_remote_copy(
            src_ref=packed.at[s, side],
            dst_ref=landed.at[s, side, slot],
            send_sem=halo_send.at[s, 2 + 3 * side + slot],
            recv_sem=halo_recv.at[s, 2 + 3 * side + slot],
            device_id={"gx": around[2 - slot], "gy": there[1 - side]},
            device_id_type=MESH,
        )

    def send_halo(s):
        for side in SIDES:
            row_copy(s, side).start()
        right = jnp.zeros((rhs, LANES), jnp.float32)
        left = jnp.zeros((rhs, LANES), jnp.float32)
        for number in range(cells):
            value = tile[s, number // rows, number % rows]
            right = jnp.where(lane == number, pltpu.roll(value, number + 1, 1), right)
            moved = pltpu.roll(value, number, 1) if number else value
            left = jnp.where(lane == number, moved, left)
        packed[s, 0] = right
        packed[s, 1] = left
        for side in SIDES:
            @pl.when(present[1 - side])
            def _():
                for slot in range(3):
                    column_copy(s, side, slot).start()

    def wait_halo(s):
        for side in SIDES:
            row_copy(s, side).wait_recv()
        for side in SIDES:
            @pl.when(present[side])
            def _():
                for slot in range(3):
                    column_copy(s, side, slot).wait_recv()

    def finish_halo(s):
        for side in SIDES:
            row_copy(s, side).wait_send()
            @pl.when(present[1 - side])
            def _():
                for slot in range(3):
                    column_copy(s, side, slot).wait_send()

    def build_shifted(s):
        for padded in range(rows + 2):
            slot = 0 if padded == 0 else 2 if padded == rows + 1 else 1
            before, after = landed[s, 0, slot], landed[s, 1, slot]
            x = (padded - 1) % rows
            for z in range(nz):
                if slot == 1:
                    value = tile[s, z, x]
                else:
                    value = ghost[s, slot // 2, z]
                number = z * rows + x
                edge = pltpu.roll(before, LANES - 1 - number, 1)
                shifted[0, z, padded] = pltpu.roll(jnp.where(lane == LANES - 1, edge, value), 1, 1)
                shifted[1, z, padded] = value
                edge = pltpu.roll(after, LANES - number, 1) if number else after
                shifted[2, z, padded] = pltpu.roll(jnp.where(lane == 0, edge, value), LANES - 1, 1)

    def apply_operator(s):
        block = s * rhs
        for z in range(nz):
            total = jnp.zeros((rows, rhs // 8, 8, LANES), jnp.float32)
            for dz in (-1, 0, 1):
                if not 0 <= z + dz < nz:
                    continue
                for dx in (-1, 0, 1):
                    for dy in (-1, 0, 1):
                        number = 9 * (dz + 1) + 3 * (dx + 1) + (dy + 1)
                        weight = wide[number, z * rows : (z + 1) * rows]
                        window = shifted[dy + 1, z + dz, 1 + dx : 1 + dx + rows]
                        total = total + weight[:, None] * window.reshape(total.shape)
            total = total.reshape(rows, rhs, LANES)
            for x in range(rows):
                here = pl.ds((z * rows + x) * LANES, LANES)
                value = total[x]
                if s > 0:
                    value = 2.0 * value - basis[pl.ds(block - rhs, rhs), here]
                basis[pl.ds(block + rhs, rhs), here] = value
                if s + 1 < STEPS:
                    tile[s + 1, z, x] = value

    def gx_copy(j, slot, x):
        return pltpu.make_async_remote_copy(
            src_ref=gram_x.at[j, slot], dst_ref=gram_x.at[j, slot],
            send_sem=gx_send.at[j, x], recv_sem=gx_recv.at[j, slot],
            device_id={"gx": x, "gy": gy}, device_id_type=MESH,
        )

    def gy_copy(j, slot, y):
        return pltpu.make_async_remote_copy(
            src_ref=gram_y.at[j, slot], dst_ref=gram_y.at[j, slot],
            send_sem=gy_send.at[j, y], recv_sem=gy_recv.at[j, slot],
            device_id={"gx": gx, "gy": y}, device_id_type=MESH,
        )

    def local_gram(j):
        upto = (j + 1) * rhs
        part = dot(basis[j * rhs : upto, :], basis[0:upto, :], NT)
        gram_x[j, gx] = jnp.concatenate(
            [part, jnp.zeros((rhs, LANES - upto), jnp.float32)], axis=1
        )
        def go(i):
            gx_copy(j, gx, lax.rem(gx + i, nx)).start()
        each(1, nx, go)

    def gram_over_gx(j):
        def wait(i):
            other = lax.rem(gx + i, nx)
            gx_copy(j, other, other).wait_recv()
        each(1, nx, wait)
        gram_y[j, gy] = jnp.sum(gram_x[j], axis=0)
        def go(i):
            gy_copy(j, gy, lax.rem(gy + i, ny)).start()
        each(1, ny, go)

    def gram_over_gy(j):
        def wait(i):
            other = lax.rem(gy + i, ny)
            gy_copy(j, other, other).wait_recv()
        each(1, ny, wait)
        return jnp.sum(gram_y[j], axis=0) / jnp.float32(total_cells)

    def finish_gram(j):
        def done_x(i):
            gx_copy(j, gx, lax.rem(gx + i, nx)).wait_send()
        each(1, nx, done_x)
        def done_y(i):
            gy_copy(j, gy, lax.rem(gy + i, ny)).wait_send()
        each(1, ny, done_y)

    def factor_block(j):
        gram = gram_over_gy(j)
        at = j * rhs
        here = slice(at, at + rhs)
        if j == 0:
            lower, inverse = factor(gram, rhs)
            l_ref[here, :] = lower
            lower_inv[here, :] = inverse
            return
        known = lower_inv[...]
        panel = jnp.where(lane < at, dot(gram, known, NT), 0.0)
        square = pltpu.roll(gram, LANES - at, 1) - jnp.concatenate(
            [dot(panel, panel, NT), jnp.zeros((rhs, LANES - rhs), jnp.float32)], axis=1
        )
        lower, inverse = factor(square, rhs)
        l_ref[here, :] = panel + pltpu.roll(lower, at, 1)
        update = dot(dot(inverse[:, :rhs], panel, NN), known, NN)
        lower_inv[here, :] = pltpu.roll(inverse, at, 1) - update

    def store(j):
        return pltpu.make_async_copy(
            out.at[j], q_hbm.at[pl.ds(j * rhs * cells, rhs * cells), :], store_sem.at[j]
        )

    def apply_block(j):
        at = j * rhs
        upto = at + rhs
        rows_j = lower_inv[at:upto, 0:upto]
        solved = dot(rows_j, basis[0:upto, :], NN)
        for number in range(cells):
            out[j, pl.ds(number, rhs, stride=cells), :] = solved[
                :, number * LANES : (number + 1) * LANES
            ]
        store(j).start()

    load_v.wait()
    for number in range(cells):
        value = v_in[pl.ds(number, rhs, stride=cells), :]
        tile[0, number // rows, number % rows] = value
        basis[0:rhs, number * LANES : (number + 1) * LANES] = value

    for s in range(STEPS):
        send_halo(s)
        if s == 0:
            load_c.wait()
            def widen(number, carry):
                values = c_in[pl.ds(number * cells, cells), :]
                center = jnp.where(number == 13, 3.0, 0.0)
                wide[number] = jnp.broadcast_to(
                    (2.0 * values - center)[:, None, :], (cells, 8, LANES)
                )
                return carry
            lax.fori_loop(0, 27, widen, 0)
        local_gram(s)
        if s >= 1:
            gram_over_gx(s - 1)
        if s >= 2:
            factor_block(s - 2)
        wait_halo(s)
        build_shifted(s)
        apply_operator(s)

    last = BLOCKS - 1
    local_gram(last)
    gram_over_gx(last - 1)
    factor_block(last - 2)
    apply_block(0)
    gram_over_gx(last)
    apply_block(1)
    apply_block(2)
    factor_block(last - 1)
    apply_block(last - 1)
    factor_block(last)
    apply_block(last)

    for s in range(STEPS):
        finish_halo(s)
    for j in range(BLOCKS):
        finish_gram(j)
        store(j).wait()


def local(nx, ny, right_sides, coefficients):
    rhs, nz, rows, columns = right_sides.shape
    cells = nz * rows
    total = BLOCKS * rhs
    f32 = jnp.float32
    solved, lower = pl.pallas_call(
        functools.partial(kernel, nx, ny, rhs, nz, rows, nx * ny * cells * columns),
        out_shape=(
            jax.ShapeDtypeStruct((total * cells, columns), f32),
            jax.ShapeDtypeStruct((total, LANES), f32),
        ),
        in_specs=[pl.BlockSpec(memory_space=pl.ANY)] * 2,
        out_specs=(pl.BlockSpec(memory_space=pl.ANY), pl.BlockSpec(memory_space=pltpu.VMEM)),
        scratch_shapes=[
            pltpu.VMEM((rhs * cells, columns), f32),
            pltpu.VMEM((27 * cells, columns), f32),
            pltpu.VMEM((27, cells, 8, LANES), f32),
            pltpu.VMEM((total, cells * LANES), f32),
            pltpu.VMEM((STEPS, nz, rows, rhs, LANES), f32),
            pltpu.VMEM((STEPS, 2, nz, rhs, LANES), f32),
            pltpu.VMEM((STEPS, 2, rhs, LANES), f32),
            pltpu.VMEM((STEPS, 2, 3, rhs, LANES), f32),
            pltpu.VMEM((3, nz, rows + 2, rhs, LANES), f32),
            pltpu.VMEM((BLOCKS, nx, rhs, LANES), f32),
            pltpu.VMEM((BLOCKS, ny, rhs, LANES), f32),
            pltpu.VMEM((LANES, LANES), f32),
            pltpu.VMEM((BLOCKS, rhs * cells, LANES), f32),
            pltpu.SemaphoreType.DMA((2,)),
            pltpu.SemaphoreType.DMA((BLOCKS,)),
            pltpu.SemaphoreType.DMA((STEPS, 8)),
            pltpu.SemaphoreType.DMA((STEPS, 8)),
            pltpu.SemaphoreType.DMA((BLOCKS, nx)),
            pltpu.SemaphoreType.DMA((BLOCKS, nx)),
            pltpu.SemaphoreType.DMA((BLOCKS, ny)),
            pltpu.SemaphoreType.DMA((BLOCKS, ny)),
        ],
        compiler_params=pltpu.CompilerParams(
            collective_id=0, has_side_effects=True, vmem_limit_bytes=40 * 1024 * 1024
        ),
    )(right_sides.reshape(rhs * cells, columns), coefficients.reshape(27 * cells, columns))
    return solved.reshape(total, nz, rows, columns), lower[:, :total].T


def solution(mesh):
    placed = (P(None, None, "gx", "gy"), P(None, None, "gx", "gy"))
    return jax.shard_map(
        functools.partial(local, mesh.shape["gx"], mesh.shape["gy"]),
        mesh=mesh,
        in_specs=placed,
        out_specs=(P(None, None, "gx", "gy"), P()),
        check_vma=False,
    )
```

time: 131 us -> 40.6 us (0.31)
  waiting for transfers between devices: 38.9 us -> 0 us
  blocking collectives: 38.7 us -> 0 us
  Pallas kernels: 0 us -> 36.4 us
  starting transfers between devices: 27.6 us -> 0 us
  other arithmetic: 18.3 us -> 0 us
  matrix products: 1.75 us -> 0 us
    ppermute x16 -> x0, waiting for transfers between devices: 38.9 us -> none  [the longest x8 28.5 us: padded_2(): before = lax.ppermute(last, axis, up)]
    psum x1 -> x0, blocking collectives: 38.7 us -> none  [local(): gram_sum = lax.psum(local_gram, ('gx', 'gy'))]
    pallas_call x0 -> x1, Pallas kernels: none -> 36.4 us  [local(): pl.pallas_call(functools.partial(kernel, nx, ny, rhs, nz, rows, nx * ny *...]
    ppermute x16 -> x0, starting transfers between devices: 27.6 us -> none  [the longest x8 24.1 us: padded_2(): after = lax.ppermute(leading, axis, down)]
    another operation x4 -> x0, other arithmetic: 14.1 us -> none  [the longest x3 7.98 us: local(): factor_lower = jnp.linalg.cholesky(gram)]
    unnamed x3 -> x0, other arithmetic: 1.94 us -> none
    slice x8 -> x0, local copies, waits for them, and re-layouts: 1.53 us -> none  [the longest x1 1.07 us: padded_2(): leading = lax.slice_in_dim(array, 0, width, axis=dim)]
    dot_general x2 -> x0, matrix products: 1.52 us -> none  [the longest x1 0.86 us: local(): solved = jnp.dot(inverse, flat, precision=lax.Precision.HIGHEST)]
  transfers between devices with their start and end apart: 16 -> 0, of which waited for: 13 -> 0; matrix products, arithmetic and copies ran while one was open for 0% -> 0% of each run, Pallas kernels for 0% -> 0%
where the time goes in v1:
time: 40.6 us; the launch traced here: 40.4 us
  Pallas kernels  36.4 us (90%)
  local copies, waits for them, and re-layouts  3.38 us (8%)
  between operations  0.66 us (2%)
    pallas_call x1, Pallas kernels, local(): pl.pallas_call(functools.partial(kernel, nx, ny, rhs, nz, rows, nx * ny *...  36.4 us
    unnamed x6, local copies, waits for them, and re-layouts  3.37 us

profile of v1, /device:TPU:0, one launch (start us, length us, event | category | flops | bytes accessed | tf_op | source)
XLA Modules:
  0.0 40.4 jit_solution(4726972425618212170)
XLA Ops:
  0.6 0.0 copy-start
  0.6 0.9 %copy-done = f32[27,4,4,128]{3,2,1,0:T(4,128)S(1)} copy-done((f32[27,4,4,128]{3,2,1,0:T(4,128)S(1)}, f32[27,4,4,128]{3,2,1,0:T(4,128)}, u32[]{:S(2)}) %copy-start) | copy-done | bytes 221208
  1.6 0.0 copy-start.1
  1.6 0.9 %copy-done.1 = f32[16,4,4,128]{3,2,1,0:T(4,128)S(1)} copy-done((f32[16,4,4,128]{3,2,1,0:T(4,128)S(1)}, f32[16,4,4,128]{3,2,1,0:T(4,128)}, u32[]{:S(2)}) %copy-start.1) | copy-done | bytes 131096
  2.5 36.4 %shard_map.41 = (f32[1280,128]{1,0:T(8,128)S(1)}, f32[80,128]{1,0:T(8,128)S(1)}) custom-call(f32[256,128]{1,0:T(8,128)S(1)} %bitcast.7, f32[432,128]{1,0:T(8,128)S(1)} %bitcast.6), custom_call_target="tpu_custom_call" | custom-call | tf_op jit(solution)/shard_map/pallas_call | solution.py:327
  38.9 0.7 %copy.4 = f32[80,80]{1,0:T(8,128)} copy(f32[80,80]{0,1:T(8,128)S(1)} %slice_bitcast_fusion) | data formatting | bytes 51200
  39.6 0.8 %copy.6 = f32[80,4,4,128]{3,2,1,0:T(4,128)} copy(f32[80,4,4,128]{3,2,1,0:T(4,128)S(1)} %bitcast.5) | data formatting | bytes 1310720
  (1 shorter events, 0.0 us)
Async XLA Ops:
  0.6 0.9 %copy-start = (f32[27,4,4,128]{3,2,1,0:T(4,128)S(1)}, f32[27,4,4,128]{3,2,1,0:T(4,128)}, u32[]{:S(2)}) copy-start(f32[27,4,4,128]{3,2,1,0:T(4,128)} %param.3) | copy-start | bytes 663556
  1.6 0.9 %copy-start.1 = (f32[16,4,4,128]{3,2,1,0:T(4,128)S(1)}, f32[16,4,4,128]{3,2,1,0:T(4,128)}, u32[]{:S(2)}) copy-start(f32[16,4,4,128]{3,2,1,0:T(4,128)} %param.2) | copy-start | bytes 393220

commit v2 on v1

--- a/solution.py
+++ b/solution.py
@@ -16,10 +16,18 @@
 NN = (((1,), (0,)), ((), ()))
 
 
-def dot(a, b, dims):
-    return lax.dot_general(
-        a, b, dims, precision=lax.Precision.HIGHEST, preferred_element_type=jnp.float32
+def split(value):
+    high = value.astype(jnp.bfloat16)
+    return high, (value - high.astype(jnp.float32)).astype(jnp.bfloat16)
+
+
+def product(a, b, dims):
+    rows = a[0].shape[0]
+    both = lax.dot_general(
+        jnp.concatenate(a, axis=0), b[0], dims, preferred_element_type=jnp.float32
     )
+    cross = lax.dot_general(a[0], b[1], dims, preferred_element_type=jnp.float32)
+    return both[:rows] + (both[rows:] + cross)
 
 
 def each(start, stop, body):
@@ -30,30 +38,72 @@
         lax.fori_loop(start, stop, lambda i, c: (body(i), c)[1], 0)
 
 
-def factor(square, rhs):
+def reciprocal(value):
+    guess = pl.reciprocal(value, approx=True)
+    guess = guess * (2.0 - value * guess)
+    return guess * (2.0 - value * guess)
+
+
+def inverse_root(value):
+    guess = lax.rsqrt(value)
+    return guess * (1.5 - 0.5 * value * guess * guess)
+
+
+def eliminate(work, at, rhs):
+    shape = work.shape
+    row = lax.broadcasted_iota(jnp.int32, shape, 0)
+    scale = jnp.zeros(shape, jnp.float32)
+    ratio = jnp.zeros(shape, jnp.float32)
+    for k in range(0, rhs, 2):
+        col0 = jnp.broadcast_to(work[:, at + k : at + k + 1], shape)
+        col1 = jnp.broadcast_to(work[:, at + k + 1 : at + k + 2], shape)
+        row0 = jnp.broadcast_to(work[k : k + 1, :], shape)
+        row1 = jnp.broadcast_to(work[k + 1 : k + 2, :], shape)
+        a = jnp.broadcast_to(col0[k : k + 1, :], shape)
+        b = jnp.broadcast_to(col1[k : k + 1, :], shape)
+        c = jnp.broadcast_to(col1[k + 1 : k + 2, :], shape)
+        over = jnp.where(row > k + 1, reciprocal(a * c - b * b), 0.0)
+        slope = b * reciprocal(a)
+        ratio = jnp.where(row == k + 1, slope, ratio)
+        scale = jnp.where(row == k, inverse_root(a), scale)
+        scale = jnp.where(row == k + 1, inverse_root(c - b * slope), scale)
+        work = work - ((c * col0 - b * col1) * row0 + (a * col1 - b * col0) * row1) * over
+    return (work - ratio * pltpu.roll(work, 1, 0)) * scale
+
+
+def factor_rows(gram, known, at, rhs, total):
     row = lax.broadcasted_iota(jnp.int32, (rhs, LANES), 0)
     lane = lax.broadcasted_iota(jnp.int32, (rhs, LANES), 1)
-    work = jnp.where(lane < rhs, square, jnp.where(lane - rhs == row, 1.0, 0.0))
-    lower = jnp.zeros((rhs, LANES), jnp.float32)
-    scale = jnp.zeros((rhs, LANES), jnp.float32)
-    for k in range(rhs):
-        column = jnp.broadcast_to(work[:, k : k + 1], (rhs, LANES))
-        pivot_row = jnp.broadcast_to(work[k : k + 1, :], (rhs, LANES))
-        pivot = jnp.broadcast_to(column[k : k + 1, :], (rhs, LANES))
-        root = 1.0 / jnp.sqrt(pivot)
-        lower = jnp.where((lane == k) & (row >= k), column * root, lower)
-        scale = jnp.where(row == k, root, scale)
-        work = work - jnp.where(row > k, column * (1.0 / pivot), 0.0) * pivot_row
-    inverse = pltpu.roll(work * scale, LANES - rhs, 1)
-    return lower, jnp.where(lane <= row, inverse, 0.0)
+    square = pltpu.roll(gram, total - at, 1) if total > at else gram
+    unit = jnp.where(lane == at + row, 1.0, 0.0)
+    if at:
+        known = split(known)
+        panel = product(split(gram), known, NT)
+        halves = split(panel)
+        done = product(halves, halves, NT)
+        done = jnp.concatenate([done, jnp.zeros((rhs, LANES - rhs), jnp.float32)], axis=1)
+        square = square - pltpu.roll(done, total, 1)
+        unit = unit - product(halves, known, NN)
+    else:
+        panel = jnp.zeros((rhs, LANES), jnp.float32)
+    work = eliminate(jnp.where(lane < total, unit, square), total, rhs)
+    inverse = jnp.where(lane < total, work, 0.0)
+    upper = jnp.where((lane >= total + row) & (lane < total + rhs), work, 0.0)
+    return panel, inverse, pltpu.roll(upper, LANES - total + at, 1)
+
+
+def put_rows(inverse_rows, high, low, out, cells):
+    rhs = inverse_rows.shape[0]
+    solved = product(split(inverse_rows), (high, low), NN)
+    for number in range(cells):
+        out[pl.ds(number, rhs, stride=cells), :] = solved[:, number * LANES : (number + 1) * LANES]
 
 
 def kernel(
     nx, ny, rhs, nz, rows, total_cells,
-    v_hbm, c_hbm, q_hbm, l_ref,
-    v_in, c_in, wide, basis, tile, ghost, packed, landed, shifted, gram_x, gram_y,
-    lower_inv, out,
-    load_sem, store_sem, halo_send, halo_recv, gx_send, gx_recv, gy_send, gy_recv,
+    v_hbm, c_hbm, high, low, out, last_gram, lower_inv, panels, upper,
+    v_in, c_in, wide, tile, ghost, packed, landed, shifted, gram_x, gram_y,
+    load_sem, halo_send, halo_recv, gx_send, gx_recv, gy_send, gy_recv,
 ):
     gx, gy = lax.axis_index("gx"), lax.axis_index("gy")
     cells = nz * rows
@@ -92,6 +142,12 @@
                 landed[s, side] = jnp.zeros((3, rhs, LANES), jnp.float32)
 
     lower_inv[...] = jnp.zeros_like(lower_inv)
+    panels[...] = jnp.zeros_like(panels)
+    upper[...] = jnp.zeros_like(upper)
+
+    def keep(j, number, value):
+        at = pl.ds(number * LANES, LANES)
+        high[pl.ds(j * rhs, rhs), at], low[pl.ds(j * rhs, rhs), at] = split(value)
 
     def row_copy(s, side):
         return pltpu.make_async_remote_copy(
@@ -166,7 +222,6 @@
                 shifted[2, z, padded] = pltpu.roll(jnp.where(lane == 0, edge, value), LANES - 1, 1)
 
     def apply_operator(s):
-        block = s * rhs
         for z in range(nz):
             total = jnp.zeros((rows, rhs // 8, 8, LANES), jnp.float32)
             for dz in (-1, 0, 1):
@@ -180,11 +235,10 @@
                         total = total + weight[:, None] * window.reshape(total.shape)
             total = total.reshape(rows, rhs, LANES)
             for x in range(rows):
-                here = pl.ds((z * rows + x) * LANES, LANES)
                 value = total[x]
                 if s > 0:
-                    value = 2.0 * value - basis[pl.ds(block - rhs, rhs), here]
-                basis[pl.ds(block + rhs, rhs), here] = value
+                    value = 2.0 * value - tile[s - 1, z, x]
+                keep(s + 1, z * rows + x, value)
                 if s + 1 < STEPS:
                     tile[s + 1, z, x] = value
 
@@ -204,7 +258,8 @@
 
     def local_gram(j):
         upto = (j + 1) * rhs
-        part = dot(basis[j * rhs : upto, :], basis[0:upto, :], NT)
+        here = slice(j * rhs, upto)
+        part = product((high[here, :], low[here, :]), (high[0:upto, :], low[0:upto, :]), NT)
         gram_x[j, gx] = jnp.concatenate(
             [part, jnp.zeros((rhs, LANES - upto), jnp.float32)], axis=1
         )
@@ -238,45 +293,24 @@
         each(1, ny, done_y)
 
     def factor_block(j):
-        gram = gram_over_gy(j)
         at = j * rhs
         here = slice(at, at + rhs)
-        if j == 0:
-            lower, inverse = factor(gram, rhs)
-            l_ref[here, :] = lower
-            lower_inv[here, :] = inverse
-            return
-        known = lower_inv[...]
-        panel = jnp.where(lane < at, dot(gram, known, NT), 0.0)
-        square = pltpu.roll(gram, LANES - at, 1) - jnp.concatenate(
-            [dot(panel, panel, NT), jnp.zeros((rhs, LANES - rhs), jnp.float32)], axis=1
-        )
-        lower, inverse = factor(square, rhs)
-        l_ref[here, :] = panel + pltpu.roll(lower, at, 1)
-        update = dot(dot(inverse[:, :rhs], panel, NN), known, NN)
-        lower_inv[here, :] = pltpu.roll(inverse, at, 1) - update
-
-    def store(j):
-        return pltpu.make_async_copy(
-            out.at[j], q_hbm.at[pl.ds(j * rhs * cells, rhs * cells), :], store_sem.at[j]
-        )
+        panel, inverse, diagonal = factor_rows(
+            gram_over_gy(j), lower_inv[...], at, rhs, BLOCKS * rhs
+        )
+        panels[here, :] = panel
+        lower_inv[here, :] = inverse
+        upper[here, :] = diagonal
 
     def apply_block(j):
-        at = j * rhs
-        upto = at + rhs
-        rows_j = lower_inv[at:upto, 0:upto]
-        solved = dot(rows_j, basis[0:upto, :], NN)
-        for number in range(cells):
-            out[j, pl.ds(number, rhs, stride=cells), :] = solved[
-                :, number * LANES : (number + 1) * LANES
-            ]
-        store(j).start()
+        at, upto = j * rhs, (j + 1) * rhs
+        put_rows(lower_inv[at:upto, 0:upto], high[0:upto, :], low[0:upto, :], out.at[j], cells)
 
     load_v.wait()
     for number in range(cells):
         value = v_in[pl.ds(number, rhs, stride=cells), :]
         tile[0, number // rows, number % rows] = value
-        basis[0:rhs, number * LANES : (number + 1) * LANES] = value
+        keep(0, number, value)
 
     for s in range(STEPS):
         send_halo(s)
@@ -309,34 +343,63 @@
     apply_block(2)
     factor_block(last - 1)
     apply_block(last - 1)
-    factor_block(last)
-    apply_block(last)
+    last_gram[...] = gram_over_gy(last)
 
     for s in range(STEPS):
         finish_halo(s)
     for j in range(BLOCKS):
         finish_gram(j)
-        store(j).wait()
+
+
+def finish_kernel(
+    rhs, cells, high, low, first, last_gram, lower_inv, panels, upper, q_hbm, r_hbm,
+    out, square, sem,
+):
+    total, last = BLOCKS * rhs, BLOCKS - 1
+    store_first = pltpu.make_async_copy(first, q_hbm.at[pl.ds(0, last), :, :], sem.at[0])
+    store_last = pltpu.make_async_copy(out, q_hbm.at[last], sem.at[1])
+    store_square = pltpu.make_async_copy(square, r_hbm, sem.at[2])
+    store_first.start()
+    at = last * rhs
+    panel, inverse, diagonal = factor_rows(last_gram[...], lower_inv[...], at, rhs, total)
+    put_rows(inverse[:, 0:total], high[...], low[...], out, cells)
+    store_last.start()
+    pad = jnp.zeros((LANES - total, LANES), jnp.float32)
+    lower = jnp.concatenate([panels[0:at, :], panel, pad], axis=0)
+    diagonals = jnp.concatenate([upper[0:at, :], diagonal, pad], axis=0)
+    square[...] = (jnp.transpose(lower) + diagonals)[0:total, 0:total]
+    store_square.start()
+    store_first.wait()
+    store_last.wait()
+    store_square.wait()
 
 
 def local(nx, ny, right_sides, coefficients):
     rhs, nz, rows, columns = right_sides.shape
     cells = nz * rows
     total = BLOCKS * rhs
-    f32 = jnp.float32
-    solved, lower = pl.pallas_call(
+    size = rhs * cells
+    f32, b16 = jnp.float32, jnp.bfloat16
+    vmem = pl.BlockSpec(memory_space=pltpu.VMEM)
+    hbm = pl.BlockSpec(memory_space=pltpu.HBM)
+    shape = jax.ShapeDtypeStruct
+    parts = pl.pallas_call(
         functools.partial(kernel, nx, ny, rhs, nz, rows, nx * ny * cells * columns),
         out_shape=(
-            jax.ShapeDtypeStruct((total * cells, columns), f32),
-            jax.ShapeDtypeStruct((total, LANES), f32),
+            shape((total, cells * LANES), b16),
+            shape((total, cells * LANES), b16),
+            shape((BLOCKS - 1, size, columns), f32),
+            shape((rhs, LANES), f32),
+            shape((LANES, LANES), f32),
+            shape((total, LANES), f32),
+            shape((total, LANES), f32),
         ),
-        in_specs=[pl.BlockSpec(memory_space=pl.ANY)] * 2,
-        out_specs=(pl.BlockSpec(memory_space=pl.ANY), pl.BlockSpec(memory_space=pltpu.VMEM)),
+        in_specs=[hbm] * 2,
+        out_specs=(vmem,) * 7,
         scratch_shapes=[
-            pltpu.VMEM((rhs * cells, columns), f32),
+            pltpu.VMEM((size, columns), f32),
             pltpu.VMEM((27 * cells, columns), f32),
             pltpu.VMEM((27, cells, 8, LANES), f32),
-            pltpu.VMEM((total, cells * LANES), f32),
             pltpu.VMEM((STEPS, nz, rows, rhs, LANES), f32),
             pltpu.VMEM((STEPS, 2, nz, rhs, LANES), f32),
             pltpu.VMEM((STEPS, 2, rhs, LANES), f32),
@@ -344,10 +407,7 @@
             pltpu.VMEM((3, nz, rows + 2, rhs, LANES), f32),
             pltpu.VMEM((BLOCKS, nx, rhs, LANES), f32),
             pltpu.VMEM((BLOCKS, ny, rhs, LANES), f32),
-            pltpu.VMEM((LANES, LANES), f32),
-            pltpu.VMEM((BLOCKS, rhs * cells, LANES), f32),
             pltpu.SemaphoreType.DMA((2,)),
-            pltpu.SemaphoreType.DMA((BLOCKS,)),
             pltpu.SemaphoreType.DMA((STEPS, 8)),
             pltpu.SemaphoreType.DMA((STEPS, 8)),
             pltpu.SemaphoreType.DMA((BLOCKS, nx)),
@@ -356,10 +416,25 @@
             pltpu.SemaphoreType.DMA((BLOCKS, ny)),
         ],
         compiler_params=pltpu.CompilerParams(
-            collective_id=0, has_side_effects=True, vmem_limit_bytes=40 * 1024 * 1024
+            collective_id=0, has_side_effects=True, vmem_limit_bytes=32 * 1024 * 1024
         ),
-    )(right_sides.reshape(rhs * cells, columns), coefficients.reshape(27 * cells, columns))
-    return solved.reshape(total, nz, rows, columns), lower[:, :total].T
+    )(
+        pltpu.with_memory_space_constraint(right_sides.reshape(size, columns), pltpu.HBM),
+        pltpu.with_memory_space_constraint(coefficients.reshape(27 * cells, columns), pltpu.HBM),
+    )
+    solved, square = pl.pallas_call(
+        functools.partial(finish_kernel, rhs, cells),
+        out_shape=(shape((BLOCKS, size, columns), f32), shape((total, total), f32)),
+        in_specs=[vmem] * 7,
+        out_specs=(hbm, hbm),
+        scratch_shapes=[
+            pltpu.VMEM((size, columns), f32),
+            pltpu.VMEM((total, total), f32),
+            pltpu.SemaphoreType.DMA((3,)),
+        ],
+        compiler_params=pltpu.CompilerParams(vmem_limit_bytes=16 * 1024 * 1024),
+    )(*parts)
+    return solved.reshape(total, nz, rows, columns), square
 
 
 def solution(mesh):

time: 40.6 us -> 33.5 us (0.83)
  Pallas kernels: 36.4 us -> 32.7 us
  local copies, waits for them, and re-layouts: 3.38 us -> 0 us
    pallas_call x1, Pallas kernels: 36.4 us -> 30.4 us  [local(): pl.pallas_call(functools.partial(kernel, nx, ny, rhs, nz, rows, nx * ny *...]
    unnamed x6 -> x0, local copies, waits for them, and re-layouts: 3.37 us -> none
    pallas_call x0 -> x1, Pallas kernels: none -> 2.28 us  [local(): pl.pallas_call(functools.partial(finish_kernel, rhs, cells), out_shape=(s...]
where the time goes in v2:
time: 33.5 us; the launch traced here: 33.3 us
  Pallas kernels  32.7 us (98%)
  between operations  0.64 us (2%)
    pallas_call x1, Pallas kernels, local(): pl.pallas_call(functools.partial(kernel, nx, ny, rhs, nz, rows, nx * ny *...  30.4 us
    pallas_call x1, Pallas kernels, local(): pl.pallas_call(functools.partial(finish_kernel, rhs, cells), out_shape=(s...  2.28 us

profile of v2, /device:TPU:0, one launch (start us, length us, event | category | flops | bytes accessed | tf_op | source)
XLA Modules:
  0.0 33.3 jit_solution(10390299092070267523)
XLA Ops:
  0.6 30.4 %shard_map.41 = (bf16[80,2048]{1,0:T(8,128)(2,1)S(1)}, bf16[80,2048]{1,0:T(8,128)(2,1)S(1)}, f32[4,256,128]{2,1,0:T(8,128)S(1)}, f32[16,128]{1,0:T(8,128)S(1)}, ...) custom-call(f32[256,128]{1,0:T(8,128)} %bitcast.4, f32[432,128]{1,0:T(8,128)} %bitcast.3), custom_call_target="tpu_custom_call" | custom-call | tf_op jit(solution)/shard_map/pallas_call | solution.py:386
  31.1 2.3 %shard_map.42 = (f32[5,256,128]{2,1,0:T(8,128)}, f32[80,80]{1,0:T(8,128)}) custom-call(bf16[80,2048]{1,0:T(8,128)(2,1)S(1)} %get-tuple-element.11.high, bf16[80,2048]{1,0:T(8,128)(2,1)S(1)} %get-tuple-element.12.low, f32[4,256,128]{2,1,0:T(8,128)S(1)} %get-tuple-element.13.first, f32[16,128]{1,0:T(8,128)S(1)} %get-tuple-element.14.last_gram, ...), custom_call_target="tpu_custom_call" | custom-call | tf_op jit(solution)/shard_map/pallas_call | solution.py:425

commit v3 on v2

--- a/solution.py
+++ b/solution.py
@@ -99,11 +99,39 @@
         out[pl.ds(number, rhs, stride=cells), :] = solved[:, number * LANES : (number + 1) * LANES]
 
 
+def turn(value, shift):
+    shift %= LANES
+    return pltpu.roll(value, shift, 1) if shift else value
+
+
+def lanes_of(value):
+    return lax.broadcasted_iota(jnp.int32, value.shape, 1)
+
+
+def edge_windows(value, left, right, number):
+    lane = lanes_of(value)
+    result = jnp.where(lane < 16, turn(right, 12 - 4 * number), 0.0)
+    result = jnp.where(lane < 12, turn(value, 12), result)
+    result = jnp.where(lane < 8, turn(value, 4), result)
+    return jnp.where(lane < 4, turn(left, -4 * number), result)
+
+
+def pack_edges(values):
+    lane = lanes_of(values[0])
+    last = first = jnp.zeros(values[0].shape, jnp.float32)
+    for number, value in enumerate(values):
+        mine = (lane >= 4 * number) & (lane < 4 * number + 4)
+        last = jnp.where(mine, turn(value, 4 * number + 4), last)
+        first = jnp.where(mine, turn(value, 4 * number), first)
+    return last, first
+
+
 def kernel(
     nx, ny, rhs, nz, rows, total_cells,
     v_hbm, c_hbm, high, low, out, last_gram, lower_inv, panels, upper,
-    v_in, c_in, wide, tile, ghost, packed, landed, shifted, gram_x, gram_y,
-    load_sem, halo_send, halo_recv, gx_send, gx_recv, gy_send, gy_recv,
+    v_in, c_in, wide, wide_edge, tile, edge, ghost, packed, landed, packed_c, landed_c,
+    packed_edge, ghost_edge, shifted, shifted_edge, gram_x, gram_y,
+    load_sem, halo_send, halo_recv, coef_send, coef_recv, gx_send, gx_recv, gy_send, gy_recv,
 ):
     gx, gy = lax.axis_index("gx"), lax.axis_index("gy")
     cells = nz * rows
@@ -118,28 +146,40 @@
     load_v.start()
     load_c.start()
 
+    pair, place = gy // 2, gy % 2
+    plane, planes = 2 * gx + place, 2 * nx
+    pairs = ny // 2
+
+    def in_plane(i):
+        other = lax.rem(plane + i, planes)
+        return other, {"gx": other // 2, "gy": 2 * pair + other % 2}
+
+    def in_line(i):
+        other = lax.rem(pair + i, pairs)
+        return other, {"gx": gx, "gy": 2 * other + place}
+
     barrier = pltpu.get_barrier_semaphore()
 
-    def greet(x, y):
-        pl.semaphore_signal(barrier, inc=1, device_id={"gx": x, "gy": y}, device_id_type=MESH)
-
-    each(1, nx, lambda i: greet(lax.rem(gx + i, nx), gy))
-    each(1, ny, lambda i: greet(gx, lax.rem(gy + i, ny)))
-    for side in SIDES:
-        @pl.when(present[side])
-        def _():
-            greet(down, there[side])
-            greet(up, there[side])
-    corners = 2 * has_left.astype(jnp.int32) + 2 * has_right.astype(jnp.int32)
-    pl.semaphore_wait(barrier, (nx - 1) + (ny - 1) + corners)
+    def greet(device):
+        pl.semaphore_signal(barrier, inc=1, device_id=device, device_id_type=MESH)
+
+    across = gy + 2 * place - 1
+    has_across = (across >= 0) & (across < ny)
+
+    @pl.when(has_across)
+    def _():
+        for x in around:
+            greet({"gx": x, "gy": across})
+    each(1, pairs, lambda i: greet(in_line(i)[1]))
+    each(1, planes, lambda i: greet(in_plane(i)[1]))
 
     lane = lax.broadcasted_iota(jnp.int32, (rhs, LANES), 1)
 
     for side in SIDES:
         @pl.when(jnp.logical_not(present[side]))
         def _():
-            for s in range(STEPS):
-                landed[s, side] = jnp.zeros((3, rhs, LANES), jnp.float32)
+            landed[side] = jnp.zeros((3, rhs, LANES), jnp.float32)
+            landed_c[side] = jnp.zeros((cells, LANES), jnp.float32)
 
     lower_inv[...] = jnp.zeros_like(lower_inv)
     panels[...] = jnp.zeros_like(panels)
@@ -159,69 +199,83 @@
             device_id_type=MESH,
         )
 
-    def column_copy(s, side, slot):
+    def column_copy(side, slot):
         return pltpu.make_async_remote_copy(
-            src_ref=packed.at[s, side],
-            dst_ref=landed.at[s, side, slot],
-            send_sem=halo_send.at[s, 2 + 3 * side + slot],
-            recv_sem=halo_recv.at[s, 2 + 3 * side + slot],
+            src_ref=packed.at[side],
+            dst_ref=landed.at[side, slot],
+            send_sem=halo_send.at[0, 2 + 3 * side + slot],
+            recv_sem=halo_recv.at[0, 2 + 3 * side + slot],
             device_id={"gx": around[2 - slot], "gy": there[1 - side]},
             device_id_type=MESH,
         )
 
-    def send_halo(s):
+    def coefficient_copy(side):
+        return pltpu.make_async_remote_copy(
+            src_ref=packed_c.at[side],
+            dst_ref=landed_c.at[side],
+            send_sem=coef_send.at[side],
+            recv_sem=coef_recv.at[side],
+            device_id={"gx": gx, "gy": there[1 - side]},
+            device_id_type=MESH,
+        )
+
+    def edge_copy(s, side):
+        return pltpu.make_async_remote_copy(
+            src_ref=packed_edge.at[s, side],
+            dst_ref=ghost_edge.at[s, side],
+            send_sem=halo_send.at[s, 2 + side],
+            recv_sem=halo_recv.at[s, 2 + side],
+            device_id={"gx": up if side == 0 else down, "gy": gy},
+            device_id_type=MESH,
+        )
+
+    def send_rows(s):
         for side in SIDES:
             row_copy(s, side).start()
-        right = jnp.zeros((rhs, LANES), jnp.float32)
-        left = jnp.zeros((rhs, LANES), jnp.float32)
-        for number in range(cells):
-            value = tile[s, number // rows, number % rows]
-            right = jnp.where(lane == number, pltpu.roll(value, number + 1, 1), right)
-            moved = pltpu.roll(value, number, 1) if number else value
-            left = jnp.where(lane == number, moved, left)
-        packed[s, 0] = right
-        packed[s, 1] = left
+
+    def send_edges(s):
+        lane8 = lax.broadcasted_iota(jnp.int32, (8, LANES), 1)
         for side in SIDES:
-            @pl.when(present[1 - side])
-            def _():
-                for slot in range(3):
-                    column_copy(s, side, slot).start()
-
-    def wait_halo(s):
-        for side in SIDES:
-            row_copy(s, side).wait_recv()
-        for side in SIDES:
-            @pl.when(present[side])
-            def _():
-                for slot in range(3):
-                    column_copy(s, side, slot).wait_recv()
-
-    def finish_halo(s):
-        for side in SIDES:
-            row_copy(s, side).wait_send()
-            @pl.when(present[1 - side])
-            def _():
-                for slot in range(3):
-                    column_copy(s, side, slot).wait_send()
+            x = rows - 1 if side == 0 else 0
+            held = jnp.zeros((8, LANES), jnp.float32)
+            for z in range(nz):
+                for half in range(rhs // 8):
+                    at = 16 * (z * (rhs // 8) + half)
+                    value = edge[s, z, x, 8 * half : 8 * half + 8, :]
+                    held = jnp.where((lane8 >= at) & (lane8 < at + 16), turn(value, at), held)
+            packed_edge[s, side] = held
+            edge_copy(s, side).start()
+
+    def ghost_edge_tile(s, side, z):
+        if s == 0:
+            slot = 2 * side
+            number = z * rows + (rows - 1 if side == 0 else 0)
+            return edge_windows(ghost[0, side, z], landed[0, slot], landed[1, slot], number)
+        held = ghost_edge[s, side]
+        per = rhs // 8
+        parts = [turn(held, -16 * (z * per + half)) for half in range(per)]
+        return jnp.concatenate(parts, axis=0)
 
     def build_shifted(s):
         for padded in range(rows + 2):
-            slot = 0 if padded == 0 else 2 if padded == rows + 1 else 1
-            before, after = landed[s, 0, slot], landed[s, 1, slot]
-            x = (padded - 1) % rows
+            x = padded - 1
             for z in range(nz):
-                if slot == 1:
-                    value = tile[s, z, x]
+                if 0 <= x < rows:
+                    value, window = tile[s, z, x], edge[s, z, x]
                 else:
-                    value = ghost[s, slot // 2, z]
-                number = z * rows + x
-                edge = pltpu.roll(before, LANES - 1 - number, 1)
-                shifted[0, z, padded] = pltpu.roll(jnp.where(lane == LANES - 1, edge, value), 1, 1)
+                    side = 0 if x < 0 else 1
+                    value, window = ghost[s, side, z], ghost_edge_tile(s, side, z)
+                shifted[0, z, padded] = jnp.where(lane == 0, turn(window, -3), turn(value, 1))
                 shifted[1, z, padded] = value
-                edge = pltpu.roll(after, LANES - number, 1) if number else after
-                shifted[2, z, padded] = pltpu.roll(jnp.where(lane == 0, edge, value), LANES - 1, 1)
-
-    def apply_operator(s):
+                shifted[2, z, padded] = jnp.where(
+                    lane == LANES - 1, turn(window, LANES - 13), turn(value, -1)
+                )
+                if s + 1 < STEPS:
+                    shifted_edge[0, z, padded] = turn(window, 1)
+                    shifted_edge[1, z, padded] = window
+                    shifted_edge[2, z, padded] = turn(window, -1)
+
+    def apply_operator(s, weights, moved, held, main):
         for z in range(nz):
             total = jnp.zeros((rows, rhs // 8, 8, LANES), jnp.float32)
             for dz in (-1, 0, 1):
@@ -230,67 +284,68 @@
                 for dx in (-1, 0, 1):
                     for dy in (-1, 0, 1):
                         number = 9 * (dz + 1) + 3 * (dx + 1) + (dy + 1)
-                        weight = wide[number, z * rows : (z + 1) * rows]
-                        window = shifted[dy + 1, z + dz, 1 + dx : 1 + dx + rows]
+                        weight = weights[number, z * rows : (z + 1) * rows]
+                        window = moved[dy + 1, z + dz, 1 + dx : 1 + dx + rows]
                         total = total + weight[:, None] * window.reshape(total.shape)
             total = total.reshape(rows, rhs, LANES)
             for x in range(rows):
                 value = total[x]
                 if s > 0:
-                    value = 2.0 * value - tile[s - 1, z, x]
-                keep(s + 1, z * rows + x, value)
+                    value = 2.0 * value - held[s - 1, z, x]
+                if main:
+                    keep(s + 1, z * rows + x, value)
                 if s + 1 < STEPS:
-                    tile[s + 1, z, x] = value
-
-    def gx_copy(j, slot, x):
+                    held[s + 1, z, x] = value
+
+    def gx_copy(j, slot, other, device):
         return pltpu.make_async_remote_copy(
             src_ref=gram_x.at[j, slot], dst_ref=gram_x.at[j, slot],
-            send_sem=gx_send.at[j, x], recv_sem=gx_recv.at[j, slot],
-            device_id={"gx": x, "gy": gy}, device_id_type=MESH,
-        )
-
-    def gy_copy(j, slot, y):
+            send_sem=gx_send.at[j, other], recv_sem=gx_recv.at[j, slot],
+            device_id=device, device_id_type=MESH,
+        )
+
+    def gy_copy(j, slot, other, device):
         return pltpu.make_async_remote_copy(
             src_ref=gram_y.at[j, slot], dst_ref=gram_y.at[j, slot],
-            send_sem=gy_send.at[j, y], recv_sem=gy_recv.at[j, slot],
-            device_id={"gx": gx, "gy": y}, device_id_type=MESH,
+            send_sem=gy_send.at[j, other], recv_sem=gy_recv.at[j, slot],
+            device_id=device, device_id_type=MESH,
         )
 
     def local_gram(j):
         upto = (j + 1) * rhs
         here = slice(j * rhs, upto)
         part = product((high[here, :], low[here, :]), (high[0:upto, :], low[0:upto, :]), NT)
-        gram_x[j, gx] = jnp.concatenate(
+        gram_x[j, plane] = jnp.concatenate(
             [part, jnp.zeros((rhs, LANES - upto), jnp.float32)], axis=1
         )
         def go(i):
-            gx_copy(j, gx, lax.rem(gx + i, nx)).start()
-        each(1, nx, go)
+            gx_copy(j, plane, *in_plane(i)).start()
+        each(1, planes, go)
 
     def gram_over_gx(j):
         def wait(i):
-            other = lax.rem(gx + i, nx)
-            gx_copy(j, other, other).wait_recv()
-        each(1, nx, wait)
-        gram_y[j, gy] = jnp.sum(gram_x[j], axis=0)
+            other, device = in_plane(i)
+            gx_copy(j, other, other, device).wait_recv()
+        each(1, planes, wait)
+        gram_y[j, pair] = jnp.sum(gram_x[j], axis=0)
         def go(i):
-            gy_copy(j, gy, lax.rem(gy + i, ny)).start()
-        each(1, ny, go)
+            gy_copy(j, pair, *in_line(i)).start()
+        each(1, pairs, go)
 
     def gram_over_gy(j):
         def wait(i):
-            other = lax.rem(gy + i, ny)
-            gy_copy(j, other, other).wait_recv()
-        each(1, ny, wait)
+            other, device = in_line(i)
+            gy_copy(j, other, other, device).wait_recv()
+        each(1, pairs, wait)
         return jnp.sum(gram_y[j], axis=0) / jnp.float32(total_cells)
 
     def finish_gram(j):
         def done_x(i):
-            gx_copy(j, gx, lax.rem(gx + i, nx)).wait_send()
-        each(1, nx, done_x)
+            gx_copy(j, plane, *in_plane(i)).wait_send()
+        each(1, planes, done_x)
         def done_y(i):
-            gy_copy(j, gy, lax.rem(gy + i, ny)).wait_send()
-        each(1, ny, done_y)
+            gy_copy(j, pair, *in_line(i)).wait_send()
+        each(1, pairs, done_y)
 
     def factor_block(j):
         at = j * rhs
@@ -307,31 +362,67 @@
         put_rows(lower_inv[at:upto, 0:upto], high[0:upto, :], low[0:upto, :], out.at[j], cells)
 
     load_v.wait()
+    values = []
     for number in range(cells):
         value = v_in[pl.ds(number, rhs, stride=cells), :]
         tile[0, number // rows, number % rows] = value
         keep(0, number, value)
+        values.append(value)
+    packed[0], packed[1] = pack_edges(values)
+
+    def weights_of(number):
+        return 2.0 * c_in[number * cells : (number + 1) * cells, :] - (3.0 if number == 13 else 0.0)
+
+    load_c.wait()
+    packed_c[0], packed_c[1] = pack_edges([weights_of(number) for number in range(27)])
+    pl.semaphore_wait(
+        barrier, (planes - 1) + (pairs - 1) + 3 * has_across.astype(jnp.int32)
+    )
+    send_rows(0)
+    for side in SIDES:
+        @pl.when(present[1 - side])
+        def _():
+            for slot in range(3):
+                column_copy(side, slot).start()
+            coefficient_copy(side).start()
+    for number in range(27):
+        wide[number] = jnp.broadcast_to(weights_of(number)[:, None, :], (cells, 8, LANES))
 
     for s in range(STEPS):
-        send_halo(s)
-        if s == 0:
-            load_c.wait()
-            def widen(number, carry):
-                values = c_in[pl.ds(number * cells, cells), :]
-                center = jnp.where(number == 13, 3.0, 0.0)
-                wide[number] = jnp.broadcast_to(
-                    (2.0 * values - center)[:, None, :], (cells, 8, LANES)
-                )
-                return carry
-            lax.fori_loop(0, 27, widen, 0)
         local_gram(s)
         if s >= 1:
             gram_over_gx(s - 1)
         if s >= 2:
             factor_block(s - 2)
-        wait_halo(s)
+        for side in SIDES:
+            row_copy(s, side).wait_recv()
+            if s > 0:
+                edge_copy(s, side).wait_recv()
+        if s == 0:
+            for side in SIDES:
+                @pl.when(present[side])
+                def _():
+                    for slot in range(3):
+                        column_copy(side, slot).wait_recv()
+            for number in range(cells):
+                z, x = number // rows, number % rows
+                edge[0, z, x] = edge_windows(tile[0, z, x], landed[0, 1], landed[1, 1], number)
         build_shifted(s)
-        apply_operator(s)
+        apply_operator(s, wide, shifted, tile, True)
+        if s + 1 < STEPS:
+            send_rows(s + 1)
+            if s == 0:
+                for side in SIDES:
+                    @pl.when(present[side])
+                    def _():
+                        coefficient_copy(side).wait_recv()
+                for number in range(27):
+                    weight = edge_windows(
+                        weights_of(number), landed_c[0], landed_c[1], number
+                    )
+                    wide_edge[number] = jnp.broadcast_to(weight[:, None, :], (cells, 8, LANES))
+            apply_operator(s, wide_edge, shifted_edge, edge, False)
+            send_edges(s + 1)
 
     last = BLOCKS - 1
     local_gram(last)
@@ -346,7 +437,16 @@
     last_gram[...] = gram_over_gy(last)
 
     for s in range(STEPS):
-        finish_halo(s)
+        for side in SIDES:
+            row_copy(s, side).wait_send()
+            if s > 0:
+                edge_copy(s, side).wait_send()
+    for side in SIDES:
+        @pl.when(present[1 - side])
+        def _():
+            for slot in range(3):
+                column_copy(side, slot).wait_send()
+            coefficient_copy(side).wait_send()
     for j in range(BLOCKS):
         finish_gram(j)
 
@@ -400,20 +500,29 @@
             pltpu.VMEM((size, columns), f32),
             pltpu.VMEM((27 * cells, columns), f32),
             pltpu.VMEM((27, cells, 8, LANES), f32),
+            pltpu.VMEM((27, cells, 8, LANES), f32),
+            pltpu.VMEM((STEPS, nz, rows, rhs, LANES), f32),
             pltpu.VMEM((STEPS, nz, rows, rhs, LANES), f32),
             pltpu.VMEM((STEPS, 2, nz, rhs, LANES), f32),
-            pltpu.VMEM((STEPS, 2, rhs, LANES), f32),
-            pltpu.VMEM((STEPS, 2, 3, rhs, LANES), f32),
+            pltpu.VMEM((2, rhs, LANES), f32),
+            pltpu.VMEM((2, 3, rhs, LANES), f32),
+            pltpu.VMEM((2, cells, LANES), f32),
+            pltpu.VMEM((2, cells, LANES), f32),
+            pltpu.VMEM((STEPS, 2, 8, LANES), f32),
+            pltpu.VMEM((STEPS, 2, 8, LANES), f32),
             pltpu.VMEM((3, nz, rows + 2, rhs, LANES), f32),
-            pltpu.VMEM((BLOCKS, nx, rhs, LANES), f32),
-            pltpu.VMEM((BLOCKS, ny, rhs, LANES), f32),
+            pltpu.VMEM((3, nz, rows + 2, rhs, LANES), f32),
+            pltpu.VMEM((BLOCKS, 2 * nx, rhs, LANES), f32),
+            pltpu.VMEM((BLOCKS, ny // 2, rhs, LANES), f32),
             pltpu.SemaphoreType.DMA((2,)),
             pltpu.SemaphoreType.DMA((STEPS, 8)),
             pltpu.SemaphoreType.DMA((STEPS, 8)),
-            pltpu.SemaphoreType.DMA((BLOCKS, nx)),
-            pltpu.SemaphoreType.DMA((BLOCKS, nx)),
-            pltpu.SemaphoreType.DMA((BLOCKS, ny)),
-            pltpu.SemaphoreType.DMA((BLOCKS, ny)),
+            pltpu.SemaphoreType.DMA((2,)),
+            pltpu.SemaphoreType.DMA((2,)),
+            pltpu.SemaphoreType.DMA((BLOCKS, 2 * nx)),
+            pltpu.SemaphoreType.DMA((BLOCKS, 2 * nx)),
+            pltpu.SemaphoreType.DMA((BLOCKS, ny // 2)),
+            pltpu.SemaphoreType.DMA((BLOCKS, ny // 2)),
         ],
         compiler_params=pltpu.CompilerParams(
             collective_id=0, has_side_effects=True, vmem_limit_bytes=32 * 1024 * 1024

time: 33.5 us -> 31.6 us (0.943)
  Pallas kernels: 32.7 us -> 30.8 us
    pallas_call x1, Pallas kernels: 30.4 us -> 28.6 us  [local(): pl.pallas_call(functools.partial(kernel, nx, ny, rhs, nz, rows, nx * ny *...]
where the time goes in v3:
time: 31.6 us; the launch traced here: 31.5 us
  Pallas kernels  30.8 us (97%)
  between operations  0.64 us (2%)
    pallas_call x1, Pallas kernels, local(): pl.pallas_call(functools.partial(kernel, nx, ny, rhs, nz, rows, nx * ny *...  28.6 us
    pallas_call x1, Pallas kernels, local(): pl.pallas_call(functools.partial(finish_kernel, rhs, cells), out_shape=(s...  2.28 us

profile of v3, /device:TPU:0, one launch (start us, length us, event | category | flops | bytes accessed | tf_op | source)
XLA Modules:
  0.0 31.5 jit_solution(17951505765881761670)
XLA Ops:
  0.6 28.6 %shard_map.41 = (bf16[80,2048]{1,0:T(8,128)(2,1)S(1)}, bf16[80,2048]{1,0:T(8,128)(2,1)S(1)}, f32[4,256,128]{2,1,0:T(8,128)S(1)}, f32[16,128]{1,0:T(8,128)S(1)}, ...) custom-call(f32[256,128]{1,0:T(8,128)} %bitcast.4, f32[432,128]{1,0:T(8,128)} %bitcast.3), custom_call_target="tpu_custom_call" | custom-call | tf_op jit(solution)/shard_map/pallas_call | solution.py:486
  29.2 2.3 %shard_map.42 = (f32[5,256,128]{2,1,0:T(8,128)}, f32[80,80]{1,0:T(8,128)}) custom-call(bf16[80,2048]{1,0:T(8,128)(2,1)S(1)} %get-tuple-element.11.high, bf16[80,2048]{1,0:T(8,128)(2,1)S(1)} %get-tuple-element.12.low, f32[4,256,128]{2,1,0:T(8,128)S(1)} %get-tuple-element.13.first, f32[16,128]{1,0:T(8,128)S(1)} %get-tuple-element.14.last_gram, ...), custom_call_target="tpu_custom_call" | custom-call | tf_op jit(solution)/shard_map/pallas_call | solution.py:534

commit v4 on v3

--- a/solution.py
+++ b/solution.py
@@ -14,6 +14,7 @@
 SIDES = (0, 1)
 NT = (((1,), (1,)), ((), ()))
 NN = (((1,), (0,)), ((), ()))
+GROUPS = ((0, 2), (2, 4), (4, 5))
 
 
 def split(value):
@@ -108,12 +109,16 @@
     return lax.broadcasted_iota(jnp.int32, value.shape, 1)
 
 
-def edge_windows(value, left, right, number):
-    lane = lanes_of(value)
-    result = jnp.where(lane < 16, turn(right, 12 - 4 * number), 0.0)
-    result = jnp.where(lane < 12, turn(value, 12), result)
-    result = jnp.where(lane < 8, turn(value, 4), result)
-    return jnp.where(lane < 4, turn(left, -4 * number), result)
+def edge_own(value, shift=0):
+    lane = (lanes_of(value) + (LANES - shift)) % LANES
+    return jnp.where(lane < 8, turn(value, 4 + shift), turn(value, 12 + shift))
+
+
+def edge_windows(own, left, right, number, shift=0):
+    lane = (lanes_of(own) + (LANES - shift)) % LANES
+    result = jnp.where(lane < 16, turn(right, 12 - 4 * number + shift), 0.0)
+    result = jnp.where(lane < 12, own, result)
+    return jnp.where(lane < 4, turn(left, shift - 4 * number), result)
 
 
 def pack_edges(values):
@@ -130,7 +135,7 @@
     nx, ny, rhs, nz, rows, total_cells,
     v_hbm, c_hbm, high, low, out, last_gram, lower_inv, panels, upper,
     v_in, c_in, wide, wide_edge, tile, edge, ghost, packed, landed, packed_c, landed_c,
-    packed_edge, ghost_edge, shifted, shifted_edge, gram_x, gram_y,
+    packed_edge, ghost_edge, padded, padded_edge, own_edge, own_c, gram_x, gram_y,
     load_sem, halo_send, halo_recv, coef_send, coef_recv, gx_send, gx_recv, gy_send, gy_recv,
 ):
     gx, gy = lax.axis_index("gx"), lax.axis_index("gy")
@@ -250,108 +255,123 @@
         if s == 0:
             slot = 2 * side
             number = z * rows + (rows - 1 if side == 0 else 0)
-            return edge_windows(ghost[0, side, z], landed[0, slot], landed[1, slot], number)
+            own = edge_own(ghost[0, side, z])
+            return edge_windows(own, landed[0, slot], landed[1, slot], number)
         held = ghost_edge[s, side]
         per = rhs // 8
         parts = [turn(held, -16 * (z * per + half)) for half in range(per)]
         return jnp.concatenate(parts, axis=0)
 
-    def build_shifted(s):
-        for padded in range(rows + 2):
-            x = padded - 1
+    def put_ghosts(s):
+        for side in SIDES:
             for z in range(nz):
-                if 0 <= x < rows:
-                    value, window = tile[s, z, x], edge[s, z, x]
-                else:
-                    side = 0 if x < 0 else 1
-                    value, window = ghost[s, side, z], ghost_edge_tile(s, side, z)
-                shifted[0, z, padded] = jnp.where(lane == 0, turn(window, -3), turn(value, 1))
-                shifted[1, z, padded] = value
-                shifted[2, z, padded] = jnp.where(
-                    lane == LANES - 1, turn(window, LANES - 13), turn(value, -1)
+                padded[z, side * (rows + 1)] = ghost[s, side, z]
+                padded_edge[z, side * (rows + 1)] = ghost_edge_tile(s, side, z)
+
+    def sums(z, weights, values, wanted):
+        parts = {dy: None for dy in wanted}
+        for dz in (-1, 0, 1):
+            if not 0 <= z + dz < nz:
+                continue
+            for dx in (-1, 0, 1):
+                window = values[z + dz, 1 + dx : 1 + dx + rows]
+                window = window.reshape(rows, rhs // 8, 8, LANES)
+                for dy in wanted:
+                    number = 9 * (dz + 1) + 3 * (dx + 1) + (dy + 1)
+                    weight = weights[number, z * rows : (z + 1) * rows]
+                    term = weight[:, None] * window
+                    parts[dy] = term if parts[dy] is None else parts[dy] + term
+        return {dy: part.reshape(rows, rhs, LANES) for dy, part in parts.items()}
+
+    def apply_operator(s):
+        more = s + 1 < STEPS
+        for z in range(nz):
+            near = sums(z, wide_edge, padded_edge, (-1, 0, 1) if more else (-1, 1))
+            here = sums(z, wide, padded, (-1, 0, 1))
+            for x in range(rows):
+                before, after = near[-1][x], near[1][x]
+                value = here[0][x]
+                value = value + jnp.where(lane == 0, turn(before, -3), turn(here[-1][x], 1))
+                value = value + jnp.where(
+                    lane == LANES - 1, turn(after, LANES - 13), turn(here[1][x], -1)
                 )
-                if s + 1 < STEPS:
-                    shifted_edge[0, z, padded] = turn(window, 1)
-                    shifted_edge[1, z, padded] = window
-                    shifted_edge[2, z, padded] = turn(window, -1)
-
-    def apply_operator(s, weights, moved, held, main):
+                if s > 0:
+                    value = 2.0 * value - tile[s - 1, z, x]
+                keep(s + 1, z * rows + x, value)
+                if more:
+                    tile[s + 1, z, x] = value
+                    value = near[0][x] + turn(before, 1) + turn(after, -1)
+                    if s > 0:
+                        value = 2.0 * value - edge[s - 1, z, x]
+                    edge[s + 1, z, x] = value
+
+    def fill_padded(s):
         for z in range(nz):
-            total = jnp.zeros((rows, rhs // 8, 8, LANES), jnp.float32)
-            for dz in (-1, 0, 1):
-                if not 0 <= z + dz < nz:
-                    continue
-                for dx in (-1, 0, 1):
-                    for dy in (-1, 0, 1):
-                        number = 9 * (dz + 1) + 3 * (dx + 1) + (dy + 1)
-                        weight = weights[number, z * rows : (z + 1) * rows]
-                        window = moved[dy + 1, z + dz, 1 + dx : 1 + dx + rows]
-                        total = total + weight[:, None] * window.reshape(total.shape)
-            total = total.reshape(rows, rhs, LANES)
             for x in range(rows):
-                value = total[x]
-                if s > 0:
-                    value = 2.0 * value - held[s - 1, z, x]
-                if main:
-                    keep(s + 1, z * rows + x, value)
-                if s + 1 < STEPS:
-                    held[s + 1, z, x] = value
-
-    def gx_copy(j, slot, other, device):
+                padded[z, 1 + x] = tile[s, z, x]
+                padded_edge[z, 1 + x] = edge[s, z, x]
+
+    def group_rows(g):
+        return pl.ds(GROUPS[g][0] * rhs, (GROUPS[g][1] - GROUPS[g][0]) * rhs)
+
+    def gx_copy(g, slot, other, device):
+        part = gram_x.at[slot, group_rows(g)]
         return pltpu.make_async_remote_copy(
-            src_ref=gram_x.at[j, slot], dst_ref=gram_x.at[j, slot],
-            send_sem=gx_send.at[j, other], recv_sem=gx_recv.at[j, slot],
+            src_ref=part, dst_ref=part,
+            send_sem=gx_send.at[g, other], recv_sem=gx_recv.at[g, slot],
             device_id=device, device_id_type=MESH,
         )
 
-    def gy_copy(j, slot, other, device):
+    def gy_copy(g, slot, other, device):
+        part = gram_y.at[slot, group_rows(g)]
         return pltpu.make_async_remote_copy(
-            src_ref=gram_y.at[j, slot], dst_ref=gram_y.at[j, slot],
-            send_sem=gy_send.at[j, other], recv_sem=gy_recv.at[j, slot],
+            src_ref=part, dst_ref=part,
+            send_sem=gy_send.at[g, other], recv_sem=gy_recv.at[g, slot],
             device_id=device, device_id_type=MESH,
         )
 
-    def local_gram(j):
-        upto = (j + 1) * rhs
-        here = slice(j * rhs, upto)
-        part = product((high[here, :], low[here, :]), (high[0:upto, :], low[0:upto, :]), NT)
-        gram_x[j, plane] = jnp.concatenate(
-            [part, jnp.zeros((rhs, LANES - upto), jnp.float32)], axis=1
+    def local_gram(g):
+        at, upto = GROUPS[g][0] * rhs, GROUPS[g][1] * rhs
+        part = product((high[at:upto, :], low[at:upto, :]), (high[0:upto, :], low[0:upto, :]), NT)
+        gram_x[plane, group_rows(g)] = jnp.concatenate(
+            [part, jnp.zeros((upto - at, LANES - upto), jnp.float32)], axis=1
         )
         def go(i):
-            gx_copy(j, plane, *in_plane(i)).start()
+            gx_copy(g, plane, *in_plane(i)).start()
         each(1, planes, go)
 
-    def gram_over_gx(j):
+    def gram_over_gx(g):
         def wait(i):
             other, device = in_plane(i)
-            gx_copy(j, other, other, device).wait_recv()
+            gx_copy(g, other, other, device).wait_recv()
         each(1, planes, wait)
-        gram_y[j, pair] = jnp.sum(gram_x[j], axis=0)
+        gram_y[pair, group_rows(g)] = jnp.sum(gram_x[:, group_rows(g)], axis=0)
         def go(i):
-            gy_copy(j, pair, *in_line(i)).start()
+            gy_copy(g, pair, *in_line(i)).start()
         each(1, pairs, go)
 
-    def gram_over_gy(j):
+    def wait_gram(g):
         def wait(i):
             other, device = in_line(i)
-            gy_copy(j, other, other, device).wait_recv()
+            gy_copy(g, other, other, device).wait_recv()
         each(1, pairs, wait)
-        return jnp.sum(gram_y[j], axis=0) / jnp.float32(total_cells)
-
-    def finish_gram(j):
+
+    def gram_block(j):
+        return jnp.sum(gram_y[:, j * rhs : (j + 1) * rhs], axis=0) / jnp.float32(total_cells)
+
+    def finish_gram(g):
         def done_x(i):
-            gx_copy(j, plane, *in_plane(i)).wait_send()
+            gx_copy(g, plane, *in_plane(i)).wait_send()
         each(1, planes, done_x)
         def done_y(i):
-            gy_copy(j, pair, *in_line(i)).wait_send()
+            gy_copy(g, pair, *in_line(i)).wait_send()
         each(1, pairs, done_y)
 
     def factor_block(j):
         at = j * rhs
         here = slice(at, at + rhs)
         panel, inverse, diagonal = factor_rows(
-            gram_over_gy(j), lower_inv[...], at, rhs, BLOCKS * rhs
+            gram_block(j), lower_inv[...], at, rhs, BLOCKS * rhs
         )
         panels[here, :] = panel
         lower_inv[here, :] = inverse
@@ -386,14 +406,24 @@
                 column_copy(side, slot).start()
             coefficient_copy(side).start()
     for number in range(27):
-        wide[number] = jnp.broadcast_to(weights_of(number)[:, None, :], (cells, 8, LANES))
-
+        weight = turn(weights_of(number), number % 3 - 1)
+        wide[number] = jnp.broadcast_to(weight[:, None, :], (cells, 8, LANES))
+        own_c[number] = edge_own(weights_of(number), number % 3 - 1)
+    for number in range(cells):
+        own_edge[number] = edge_own(tile[0, number // rows, number % rows])
+
+    last = BLOCKS - 1
     for s in range(STEPS):
-        local_gram(s)
-        if s >= 1:
-            gram_over_gx(s - 1)
-        if s >= 2:
-            factor_block(s - 2)
+        if s == 1:
+            local_gram(0)
+        if s == 2:
+            gram_over_gx(0)
+        if s == 3:
+            local_gram(1)
+            wait_gram(0)
+            factor_block(0)
+        if s > 0:
+            fill_padded(s)
         for side in SIDES:
             row_copy(s, side).wait_recv()
             if s > 0:
@@ -402,40 +432,30 @@
             for side in SIDES:
                 @pl.when(present[side])
                 def _():
+                    coefficient_copy(side).wait_recv()
                     for slot in range(3):
                         column_copy(side, slot).wait_recv()
             for number in range(cells):
                 z, x = number // rows, number % rows
-                edge[0, z, x] = edge_windows(tile[0, z, x], landed[0, 1], landed[1, 1], number)
-        build_shifted(s)
-        apply_operator(s, wide, shifted, tile, True)
+                edge[0, z, x] = edge_windows(own_edge[number], landed[0, 1], landed[1, 1], number)
+            for number in range(27):
+                weight = edge_windows(
+                    own_c[number], landed_c[0], landed_c[1], number, number % 3 - 1
+                )
+                wide_edge[number] = jnp.broadcast_to(weight[:, None, :], (cells, 8, LANES))
+            fill_padded(s)
+        put_ghosts(s)
+        apply_operator(s)
         if s + 1 < STEPS:
             send_rows(s + 1)
-            if s == 0:
-                for side in SIDES:
-                    @pl.when(present[side])
-                    def _():
-                        coefficient_copy(side).wait_recv()
-                for number in range(27):
-                    weight = edge_windows(
-                        weights_of(number), landed_c[0], landed_c[1], number
-                    )
-                    wide_edge[number] = jnp.broadcast_to(weight[:, None, :], (cells, 8, LANES))
-            apply_operator(s, wide_edge, shifted_edge, edge, False)
             send_edges(s + 1)
 
-    last = BLOCKS - 1
-    local_gram(last)
-    gram_over_gx(last - 1)
-    factor_block(last - 2)
+    local_gram(2)
+    gram_over_gx(1)
+    factor_block(1)
     apply_block(0)
-    gram_over_gx(last)
     apply_block(1)
-    apply_block(2)
-    factor_block(last - 1)
-    apply_block(last - 1)
-    last_gram[...] = gram_over_gy(last)
-
+    gram_over_gx(2)
     for s in range(STEPS):
         for side in SIDES:
             row_copy(s, side).wait_send()
@@ -447,8 +467,16 @@
             for slot in range(3):
                 column_copy(side, slot).wait_send()
             coefficient_copy(side).wait_send()
-    for j in range(BLOCKS):
-        finish_gram(j)
+    finish_gram(0)
+    wait_gram(1)
+    factor_block(2)
+    apply_block(2)
+    factor_block(3)
+    apply_block(3)
+    finish_gram(1)
+    wait_gram(2)
+    last_gram[...] = gram_block(last)
+    finish_gram(2)
 
 
 def finish_kernel(
@@ -510,19 +538,21 @@
             pltpu.VMEM((2, cells, LANES), f32),
             pltpu.VMEM((STEPS, 2, 8, LANES), f32),
             pltpu.VMEM((STEPS, 2, 8, LANES), f32),
-            pltpu.VMEM((3, nz, rows + 2, rhs, LANES), f32),
-            pltpu.VMEM((3, nz, rows + 2, rhs, LANES), f32),
-            pltpu.VMEM((BLOCKS, 2 * nx, rhs, LANES), f32),
-            pltpu.VMEM((BLOCKS, ny // 2, rhs, LANES), f32),
+            pltpu.VMEM((nz, rows + 2, rhs, LANES), f32),
+            pltpu.VMEM((nz, rows + 2, rhs, LANES), f32),
+            pltpu.VMEM((cells, rhs, LANES), f32),
+            pltpu.VMEM((27, cells, LANES), f32),
+            pltpu.VMEM((2 * nx, total, LANES), f32),
+            pltpu.VMEM((ny // 2, total, LANES), f32),
             pltpu.SemaphoreType.DMA((2,)),
             pltpu.SemaphoreType.DMA((STEPS, 8)),
             pltpu.SemaphoreType.DMA((STEPS, 8)),
             pltpu.SemaphoreType.DMA((2,)),
             pltpu.SemaphoreType.DMA((2,)),
-            pltpu.SemaphoreType.DMA((BLOCKS, 2 * nx)),
-            pltpu.SemaphoreType.DMA((BLOCKS, 2 * nx)),
-            pltpu.SemaphoreType.DMA((BLOCKS, ny // 2)),
-            pltpu.SemaphoreType.DMA((BLOCKS, ny // 2)),
+            pltpu.SemaphoreType.DMA((len(GROUPS), 2 * nx)),
+            pltpu.SemaphoreType.DMA((len(GROUPS), 2 * nx)),
+            pltpu.SemaphoreType.DMA((len(GROUPS), ny // 2)),
+            pltpu.SemaphoreType.DMA((len(GROUPS), ny // 2)),
         ],
         compiler_params=pltpu.CompilerParams(
             collective_id=0, has_side_effects=True, vmem_limit_bytes=32 * 1024 * 1024

time: 31.6 us -> 31.6 us (level)
  no operation moved by 1% of the time
where the time goes in v4:
time: 31.6 us; the launch traced here: 31.5 us
  Pallas kernels  30.8 us (97%)
  between operations  0.64 us (2%)
    pallas_call x1, Pallas kernels, local(): pl.pallas_call(functools.partial(kernel, nx, ny, rhs, nz, rows, nx * ny *...  28.5 us
    pallas_call x1, Pallas kernels, local(): pl.pallas_call(functools.partial(finish_kernel, rhs, cells), out_shape=(s...  2.28 us

profile of v4, /device:TPU:0, one launch (start us, length us, event | category | flops | bytes accessed | tf_op | source)
XLA Modules:
  0.0 31.5 jit_solution(10824102844409559445)
XLA Ops:
  0.6 28.5 %shard_map.41 = (bf16[80,2048]{1,0:T(8,128)(2,1)S(1)}, bf16[80,2048]{1,0:T(8,128)(2,1)S(1)}, f32[4,256,128]{2,1,0:T(8,128)S(1)}, f32[16,128]{1,0:T(8,128)S(1)}, ...) custom-call(f32[256,128]{1,0:T(8,128)} %bitcast.4, f32[432,128]{1,0:T(8,128)} %bitcast.3), custom_call_target="tpu_custom_call" | custom-call | tf_op jit(solution)/shard_map/pallas_call | solution.py:514
  29.2 2.3 %shard_map.42 = (f32[5,256,128]{2,1,0:T(8,128)}, f32[80,80]{1,0:T(8,128)}) custom-call(bf16[80,2048]{1,0:T(8,128)(2,1)S(1)} %get-tuple-element.11.high, bf16[80,2048]{1,0:T(8,128)(2,1)S(1)} %get-tuple-element.12.low, f32[4,256,128]{2,1,0:T(8,128)S(1)} %get-tuple-element.13.first, f32[16,128]{1,0:T(8,128)S(1)} %get-tuple-element.14.last_gram, ...), custom_call_target="tpu_custom_call" | custom-call | tf_op jit(solution)/shard_map/pallas_call | solution.py:564

commit v5 on v4

--- a/solution.py
+++ b/solution.py
@@ -93,16 +93,20 @@
     return panel, inverse, pltpu.roll(upper, LANES - total + at, 1)
 
 
-def put_rows(inverse_rows, high, low, out, cells):
-    rhs = inverse_rows.shape[0]
-    solved = product(split(inverse_rows), (high, low), NN)
-    for number in range(cells):
-        out[pl.ds(number, rhs, stride=cells), :] = solved[:, number * LANES : (number + 1) * LANES]
+def put_rows(lines, high, low, out, first, rhs, cells):
+    solved = product(split(lines), (high, low), NN)
+    for block in range(lines.shape[0] // rhs):
+        for number in range(cells):
+            out[first + block, pl.ds(number, rhs, stride=cells), :] = solved[
+                block * rhs : (block + 1) * rhs, number * LANES : (number + 1) * LANES
+            ]
 
 
 def turn(value, shift):
-    shift %= LANES
-    return pltpu.roll(value, shift, 1) if shift else value
+    if isinstance(shift, int):
+        shift %= LANES
+        return pltpu.roll(value, shift, 1) if shift else value
+    return pltpu.roll(value, lax.rem(shift + 8 * LANES, LANES), 1)
 
 
 def lanes_of(value):
@@ -121,14 +125,23 @@
     return jnp.where(lane < 4, turn(left, shift - 4 * number), result)
 
 
-def pack_edges(values):
-    lane = lanes_of(values[0])
-    last = first = jnp.zeros(values[0].shape, jnp.float32)
-    for number, value in enumerate(values):
-        mine = (lane >= 4 * number) & (lane < 4 * number + 4)
-        last = jnp.where(mine, turn(value, 4 * number + 4), last)
-        first = jnp.where(mine, turn(value, 4 * number), first)
-    return last, first
+def pack_edges(count, unroll, get, shape):
+    def more(step, held):
+        last, first = held
+        for part in range(unroll):
+            number = step * unroll + part
+            value = get(number)
+            lane = lanes_of(value)
+            mine = (lane >= 4 * number) & (lane < 4 * number + 4)
+            last = jnp.where(mine, turn(value, 4 * number + 4), last)
+            first = jnp.where(mine, turn(value, 4 * number), first)
+        return last, first
+    zero = jnp.zeros(shape, jnp.float32)
+    return lax.fori_loop(0, count // unroll, more, (zero, zero))
+
+
+def loop(count, body):
+    lax.fori_loop(0, count, lambda i, c: (body(i), c)[1], 0)
 
 
 def kernel(
@@ -190,9 +203,16 @@
     panels[...] = jnp.zeros_like(panels)
     upper[...] = jnp.zeros_like(upper)
 
+    for plane_out in (0, nz + 1):
+        padded[plane_out] = jnp.zeros((rows + 2, rhs, LANES), jnp.float32)
+        padded_edge[plane_out] = jnp.zeros((rows + 2, rhs, LANES), jnp.float32)
+
     def keep(j, number, value):
-        at = pl.ds(number * LANES, LANES)
-        high[pl.ds(j * rhs, rhs), at], low[pl.ds(j * rhs, rhs), at] = split(value)
+        at = pl.ds(pl.multiple_of(number * LANES, LANES), LANES)
+        high[j, :, at], low[j, :, at] = split(value)
+
+    def flat(ref, start, stop):
+        return ref[start:stop].reshape((stop - start) * rhs, cells * LANES)
 
     def row_copy(s, side):
         return pltpu.make_async_remote_copy(
@@ -251,43 +271,51 @@
             packed_edge[s, side] = held
             edge_copy(s, side).start()
 
-    def ghost_edge_tile(s, side, z):
-        if s == 0:
-            slot = 2 * side
-            number = z * rows + (rows - 1 if side == 0 else 0)
-            own = edge_own(ghost[0, side, z])
-            return edge_windows(own, landed[0, slot], landed[1, slot], number)
-        held = ghost_edge[s, side]
-        per = rhs // 8
-        parts = [turn(held, -16 * (z * per + half)) for half in range(per)]
-        return jnp.concatenate(parts, axis=0)
-
     def put_ghosts(s):
         for side in SIDES:
+            at = side * (rows + 1)
             for z in range(nz):
-                padded[z, side * (rows + 1)] = ghost[s, side, z]
-                padded_edge[z, side * (rows + 1)] = ghost_edge_tile(s, side, z)
-
-    def sums(z, weights, values, wanted):
-        parts = {dy: None for dy in wanted}
+                padded[z + 1, at] = ghost[s, side, z]
+
+            @pl.when(s == 0)
+            def _():
+                slot = 2 * side
+                def put(z):
+                    number = z * rows + (rows - 1 if side == 0 else 0)
+                    own = edge_own(ghost[0, side, z])
+                    padded_edge[z + 1, at] = edge_windows(
+                        own, landed[0, slot], landed[1, slot], number
+                    )
+                loop(nz, put)
+
+            @pl.when(s > 0)
+            def _():
+                held = ghost_edge[s, side]
+                per = rhs // 8
+                for z in range(nz):
+                    parts = [turn(held, -16 * (z * per + half)) for half in range(per)]
+                    padded_edge[z + 1, at] = jnp.concatenate(parts, axis=0)
+
+    def sums(z, weights, values):
+        parts = {}
         for dz in (-1, 0, 1):
-            if not 0 <= z + dz < nz:
-                continue
             for dx in (-1, 0, 1):
-                window = values[z + dz, 1 + dx : 1 + dx + rows]
+                window = values[z + 1 + dz, 1 + dx : 1 + dx + rows]
                 window = window.reshape(rows, rhs // 8, 8, LANES)
-                for dy in wanted:
+                for dy in (-1, 0, 1):
                     number = 9 * (dz + 1) + 3 * (dx + 1) + (dy + 1)
-                    weight = weights[number, z * rows : (z + 1) * rows]
-                    term = weight[:, None] * window
-                    parts[dy] = term if parts[dy] is None else parts[dy] + term
+                    term = weights[number, z][:, None] * window
+                    parts[dy] = parts[dy] + term if dy in parts else term
         return {dy: part.reshape(rows, rhs, LANES) for dy, part in parts.items()}
 
     def apply_operator(s):
-        more = s + 1 < STEPS
-        for z in range(nz):
-            near = sums(z, wide_edge, padded_edge, (-1, 0, 1) if more else (-1, 1))
-            here = sums(z, wide, padded, (-1, 0, 1))
+        factor_now = jnp.where(s > 0, 2.0, 1.0)
+        factor_before = jnp.where(s > 0, 1.0, 0.0)
+        before_s = jnp.maximum(s - 1, 0)
+
+        def plane_of(z):
+            near = sums(z, wide_edge, padded_edge)
+            here = sums(z, wide, padded)
             for x in range(rows):
                 before, after = near[-1][x], near[1][x]
                 value = here[0][x]
@@ -295,21 +323,18 @@
                 value = value + jnp.where(
                     lane == LANES - 1, turn(after, LANES - 13), turn(here[1][x], -1)
                 )
-                if s > 0:
-                    value = 2.0 * value - tile[s - 1, z, x]
+                value = factor_now * value - factor_before * tile[before_s, z, x]
                 keep(s + 1, z * rows + x, value)
-                if more:
-                    tile[s + 1, z, x] = value
-                    value = near[0][x] + turn(before, 1) + turn(after, -1)
-                    if s > 0:
-                        value = 2.0 * value - edge[s - 1, z, x]
-                    edge[s + 1, z, x] = value
+                tile[s + 1, z, x] = value
+                value = near[0][x] + turn(before, 1) + turn(after, -1)
+                edge[s + 1, z, x] = factor_now * value - factor_before * edge[before_s, z, x]
+        loop(nz, plane_of)
 
     def fill_padded(s):
         for z in range(nz):
             for x in range(rows):
-                padded[z, 1 + x] = tile[s, z, x]
-                padded_edge[z, 1 + x] = edge[s, z, x]
+                padded[z + 1, 1 + x] = tile[s, z, x]
+                padded_edge[z + 1, 1 + x] = edge[s, z, x]
 
     def group_rows(g):
         return pl.ds(GROUPS[g][0] * rhs, (GROUPS[g][1] - GROUPS[g][0]) * rhs)
@@ -332,7 +357,12 @@
 
     def local_gram(g):
         at, upto = GROUPS[g][0] * rhs, GROUPS[g][1] * rhs
-        part = product((high[at:upto, :], low[at:upto, :]), (high[0:upto, :], low[0:upto, :]), NT)
+        first, stop = GROUPS[g]
+        part = product(
+            (flat(high, first, stop), flat(low, first, stop)),
+            (flat(high, 0, stop), flat(low, 0, stop)),
+            NT,
+        )
         gram_x[plane, group_rows(g)] = jnp.concatenate(
             [part, jnp.zeros((upto - at, LANES - upto), jnp.float32)], axis=1
         )
@@ -377,24 +407,31 @@
         lower_inv[here, :] = inverse
         upper[here, :] = diagonal
 
-    def apply_block(j):
-        at, upto = j * rhs, (j + 1) * rhs
-        put_rows(lower_inv[at:upto, 0:upto], high[0:upto, :], low[0:upto, :], out.at[j], cells)
+    def apply_blocks(start, stop):
+        lines = lower_inv[start * rhs : stop * rhs, 0 : stop * rhs]
+        put_rows(lines, flat(high, 0, stop), flat(low, 0, stop), out, start, rhs, cells)
 
     load_v.wait()
-    values = []
-    for number in range(cells):
+
+    def take(number):
         value = v_in[pl.ds(number, rhs, stride=cells), :]
         tile[0, number // rows, number % rows] = value
         keep(0, number, value)
-        values.append(value)
-    packed[0], packed[1] = pack_edges(values)
+    for number in range(cells):
+        take(number)
+    packed[0], packed[1] = pack_edges(
+        cells, 4, lambda number: tile[0, number // rows, number % rows], (rhs, LANES)
+    )
 
     def weights_of(number):
-        return 2.0 * c_in[number * cells : (number + 1) * cells, :] - (3.0 if number == 13 else 0.0)
+        values = c_in[pl.ds(pl.multiple_of(number * cells, cells), cells), :]
+        return 2.0 * values - jnp.where(number == 13, 3.0, 0.0)
+
+    def widened(value):
+        return jnp.broadcast_to(value[:, None, :], (cells, 8, LANES)).reshape(nz, rows, 8, LANES)
 
     load_c.wait()
-    packed_c[0], packed_c[1] = pack_edges([weights_of(number) for number in range(27)])
+    packed_c[0], packed_c[1] = pack_edges(27, 3, weights_of, (cells, LANES))
     pl.semaphore_wait(
         barrier, (planes - 1) + (pairs - 1) + 3 * has_across.astype(jnp.int32)
     )
@@ -405,56 +442,72 @@
             for slot in range(3):
                 column_copy(side, slot).start()
             coefficient_copy(side).start()
-    for number in range(27):
-        weight = turn(weights_of(number), number % 3 - 1)
-        wide[number] = jnp.broadcast_to(weight[:, None, :], (cells, 8, LANES))
-        own_c[number] = edge_own(weights_of(number), number % 3 - 1)
+
+    def prepare(step):
+        for part in range(3):
+            number = 3 * step + part
+            wide[number] = widened(turn(weights_of(number), part - 1))
+            own_c[number] = edge_own(weights_of(number), part - 1)
+    loop(9, prepare)
     for number in range(cells):
         own_edge[number] = edge_own(tile[0, number // rows, number % rows])
 
+    for side in SIDES:
+        @pl.when(present[side])
+        def _():
+            coefficient_copy(side).wait_recv()
+            for slot in range(3):
+                column_copy(side, slot).wait_recv()
+
+    def join_edge(step):
+        for part in range(4):
+            number = 4 * step + part
+            edge[0, number // rows, number % rows] = edge_windows(
+                own_edge[number], landed[0, 1], landed[1, 1], number
+            )
+    loop(cells // 4, join_edge)
+
+    def join_weights(step):
+        for part in range(3):
+            number = 3 * step + part
+            wide_edge[number] = widened(
+                edge_windows(own_c[number], landed_c[0], landed_c[1], number, part - 1)
+            )
+    loop(9, join_weights)
+
     last = BLOCKS - 1
-    for s in range(STEPS):
-        if s == 1:
+
+    def step_of(s):
+        @pl.when(s == 1)
+        def _():
             local_gram(0)
-        if s == 2:
+        @pl.when(s == 2)
+        def _():
             gram_over_gx(0)
-        if s == 3:
+        @pl.when(s == 3)
+        def _():
             local_gram(1)
             wait_gram(0)
             factor_block(0)
-        if s > 0:
-            fill_padded(s)
+        fill_padded(s)
         for side in SIDES:
             row_copy(s, side).wait_recv()
-            if s > 0:
+            @pl.when(s > 0)
+            def _():
                 edge_copy(s, side).wait_recv()
-        if s == 0:
-            for side in SIDES:
-                @pl.when(present[side])
-                def _():
-                    coefficient_copy(side).wait_recv()
-                    for slot in range(3):
-                        column_copy(side, slot).wait_recv()
-            for number in range(cells):
-                z, x = number // rows, number % rows
-                edge[0, z, x] = edge_windows(own_edge[number], landed[0, 1], landed[1, 1], number)
-            for number in range(27):
-                weight = edge_windows(
-                    own_c[number], landed_c[0], landed_c[1], number, number % 3 - 1
-                )
-                wide_edge[number] = jnp.broadcast_to(weight[:, None, :], (cells, 8, LANES))
-            fill_padded(s)
         put_ghosts(s)
         apply_operator(s)
-        if s + 1 < STEPS:
+
+        @pl.when(s + 1 < STEPS)
+        def _():
             send_rows(s + 1)
             send_edges(s + 1)
+    loop(STEPS, step_of)
 
     local_gram(2)
     gram_over_gx(1)
     factor_block(1)
-    apply_block(0)
-    apply_block(1)
+    apply_blocks(0, 2)
     gram_over_gx(2)
     for s in range(STEPS):
         for side in SIDES:
@@ -470,9 +523,8 @@
     finish_gram(0)
     wait_gram(1)
     factor_block(2)
-    apply_block(2)
     factor_block(3)
-    apply_block(3)
+    apply_blocks(2, 4)
     finish_gram(1)
     wait_gram(2)
     last_gram[...] = gram_block(last)
@@ -485,12 +537,13 @@
 ):
     total, last = BLOCKS * rhs, BLOCKS - 1
     store_first = pltpu.make_async_copy(first, q_hbm.at[pl.ds(0, last), :, :], sem.at[0])
-    store_last = pltpu.make_async_copy(out, q_hbm.at[last], sem.at[1])
+    store_last = pltpu.make_async_copy(out.at[0], q_hbm.at[last], sem.at[1])
     store_square = pltpu.make_async_copy(square, r_hbm, sem.at[2])
     store_first.start()
     at = last * rhs
     panel, inverse, diagonal = factor_rows(last_gram[...], lower_inv[...], at, rhs, total)
-    put_rows(inverse[:, 0:total], high[...], low[...], out, cells)
+    shape = (total, cells * LANES)
+    put_rows(inverse[:, 0:total], high[...].reshape(shape), low[...].reshape(shape), out, 0, rhs, cells)
     store_last.start()
     pad = jnp.zeros((LANES - total, LANES), jnp.float32)
     lower = jnp.concatenate([panels[0:at, :], panel, pad], axis=0)
@@ -514,8 +567,8 @@
     parts = pl.pallas_call(
         functools.partial(kernel, nx, ny, rhs, nz, rows, nx * ny * cells * columns),
         out_shape=(
-            shape((total, cells * LANES), b16),
-            shape((total, cells * LANES), b16),
+            shape((BLOCKS, rhs, cells * LANES), b16),
+            shape((BLOCKS, rhs, cells * LANES), b16),
             shape((BLOCKS - 1, size, columns), f32),
             shape((rhs, LANES), f32),
             shape((LANES, LANES), f32),
@@ -527,10 +580,10 @@
         scratch_shapes=[
             pltpu.VMEM((size, columns), f32),
             pltpu.VMEM((27 * cells, columns), f32),
-            pltpu.VMEM((27, cells, 8, LANES), f32),
-            pltpu.VMEM((27, cells, 8, LANES), f32),
-            pltpu.VMEM((STEPS, nz, rows, rhs, LANES), f32),
-            pltpu.VMEM((STEPS, nz, rows, rhs, LANES), f32),
+            pltpu.VMEM((27, nz, rows, 8, LANES), f32),
+            pltpu.VMEM((27, nz, rows, 8, LANES), f32),
+            pltpu.VMEM((BLOCKS, nz, rows, rhs, LANES), f32),
+            pltpu.VMEM((BLOCKS, nz, rows, rhs, LANES), f32),
             pltpu.VMEM((STEPS, 2, nz, rhs, LANES), f32),
             pltpu.VMEM((2, rhs, LANES), f32),
             pltpu.VMEM((2, 3, rhs, LANES), f32),
@@ -538,8 +591,8 @@
             pltpu.VMEM((2, cells, LANES), f32),
             pltpu.VMEM((STEPS, 2, 8, LANES), f32),
             pltpu.VMEM((STEPS, 2, 8, LANES), f32),
-            pltpu.VMEM((nz, rows + 2, rhs, LANES), f32),
-            pltpu.VMEM((nz, rows + 2, rhs, LANES), f32),
+            pltpu.VMEM((nz + 2, rows + 2, rhs, LANES), f32),
+            pltpu.VMEM((nz + 2, rows + 2, rhs, LANES), f32),
             pltpu.VMEM((cells, rhs, LANES), f32),
             pltpu.VMEM((27, cells, LANES), f32),
             pltpu.VMEM((2 * nx, total, LANES), f32),
@@ -567,7 +620,7 @@
         in_specs=[vmem] * 7,
         out_specs=(hbm, hbm),
         scratch_shapes=[
-            pltpu.VMEM((size, columns), f32),
+            pltpu.VMEM((1, size, columns), f32),
             pltpu.VMEM((total, total), f32),
             pltpu.SemaphoreType.DMA((3,)),
         ],

time: 31.6 us -> 34.2 us (1.082)
  Pallas kernels: 30.8 us -> 33.4 us
    pallas_call x1, Pallas kernels: 28.5 us -> 31.2 us  [local(): pl.pallas_call(functools.partial(kernel, nx, ny, rhs, nz, rows, nx * ny *...]
where the time goes in v5:
time: 34.2 us; the launch traced here: 34.1 us
  Pallas kernels  33.4 us (98%)
  between operations  0.64 us (2%)
    pallas_call x1, Pallas kernels, local(): pl.pallas_call(functools.partial(kernel, nx, ny, rhs, nz, rows, nx * ny *...  31.2 us
    pallas_call x1, Pallas kernels, local(): pl.pallas_call(functools.partial(finish_kernel, rhs, cells), out_shape=(s...  2.28 us

profile of v5, /device:TPU:0, one launch (start us, length us, event | category | flops | bytes accessed | tf_op | source)
XLA Modules:
  0.0 34.1 jit_solution(279509584545046032)
XLA Ops:
  0.6 31.2 %shard_map.41 = (bf16[5,16,2048]{2,1,0:T(8,128)(2,1)S(1)}, bf16[5,16,2048]{2,1,0:T(8,128)(2,1)S(1)}, f32[4,256,128]{2,1,0:T(8,128)S(1)}, f32[16,128]{1,0:T(8,128...) custom-call(f32[256,128]{1,0:T(8,128)} %bitcast.4, f32[432,128]{1,0:T(8,128)} %bitcast.3), custom_call_target="tpu_custom_call" | custom-call | tf_op jit(solution)/shard_map/pallas_call | solution.py:567
  31.8 2.3 %shard_map.42 = (f32[5,256,128]{2,1,0:T(8,128)}, f32[80,80]{1,0:T(8,128)}) custom-call(bf16[5,16,2048]{2,1,0:T(8,128)(2,1)S(1)} %get-tuple-element.11.high, bf16[5,16,2048]{2,1,0:T(8,128)(2,1)S(1)} %get-tuple-element.12.low, f32[4,256,128]{2,1,0:T(8,128)S(1)} %get-tuple-element.13.first, f32[16,128]{1,0:T(8,128)S(1)} %get-tuple-element.14.last_gram, ...), custom_call_target="tpu_custom_call" | custom-call | tf_op jit(solution)/shard_map/pallas_call | solution.py:617

commit v6 on v4

--- a/solution.py
+++ b/solution.py
@@ -246,70 +246,97 @@
             for z in range(nz):
                 for half in range(rhs // 8):
                     at = 16 * (z * (rhs // 8) + half)
-                    value = edge[s, z, x, 8 * half : 8 * half + 8, :]
-                    held = jnp.where((lane8 >= at) & (lane8 < at + 16), turn(value, at), held)
+                    value = turn(edge[s, z, 8 * half : 8 * half + 8, :], at - 16 * (x + 1))
+                    held = jnp.where((lane8 >= at) & (lane8 < at + 16), value, held)
             packed_edge[s, side] = held
             edge_copy(s, side).start()
 
-    def ghost_edge_tile(s, side, z):
+    def ghost_window(s, side, z):
+        at = 16 * side * (rows + 1)
         if s == 0:
             slot = 2 * side
             number = z * rows + (rows - 1 if side == 0 else 0)
-            own = edge_own(ghost[0, side, z])
-            return edge_windows(own, landed[0, slot], landed[1, slot], number)
+            own = edge_own(ghost[0, side, z], at)
+            return edge_windows(own, landed[0, slot], landed[1, slot], number, at)
         held = ghost_edge[s, side]
         per = rhs // 8
-        parts = [turn(held, -16 * (z * per + half)) for half in range(per)]
+        parts = [turn(held, at - 16 * (z * per + half)) for half in range(per)]
         return jnp.concatenate(parts, axis=0)
 
     def put_ghosts(s):
-        for side in SIDES:
-            for z in range(nz):
-                padded[z, side * (rows + 1)] = ghost[s, side, z]
-                padded_edge[z, side * (rows + 1)] = ghost_edge_tile(s, side, z)
-
-    def sums(z, weights, values, wanted):
-        parts = {dy: None for dy in wanted}
+        for z in range(nz):
+            window = edge[s, z]
+            for side in SIDES:
+                at = side * (rows + 1)
+                padded[z, at] = ghost[s, side, z]
+                there_lane = (lane >= 16 * at) & (lane < 16 * at + 16)
+                window = jnp.where(there_lane, ghost_window(s, side, z), window)
+            padded_edge[z] = window
+
+    def sums(z):
+        parts = {}
         for dz in (-1, 0, 1):
             if not 0 <= z + dz < nz:
                 continue
             for dx in (-1, 0, 1):
-                window = values[z + dz, 1 + dx : 1 + dx + rows]
+                window = padded[z + dz, 1 + dx : 1 + dx + rows]
                 window = window.reshape(rows, rhs // 8, 8, LANES)
-                for dy in wanted:
+                for dy in (-1, 0, 1):
                     number = 9 * (dz + 1) + 3 * (dx + 1) + (dy + 1)
-                    weight = weights[number, z * rows : (z + 1) * rows]
+                    weight = wide[number, z * rows : (z + 1) * rows]
                     term = weight[:, None] * window
-                    parts[dy] = term if parts[dy] is None else parts[dy] + term
+                    parts[dy] = parts[dy] + term if dy in parts else term
         return {dy: part.reshape(rows, rhs, LANES) for dy, part in parts.items()}
+
+    def edge_sums(z, wanted):
+        result = {}
+        for dy in wanted:
+            total = None
+            for dx in (-1, 0, 1):
+                part = None
+                for dz in (-1, 0, 1):
+                    if not 0 <= z + dz < nz:
+                        continue
+                    number = 9 * (dz + 1) + 3 * (dx + 1) + (dy + 1)
+                    term = wide_edge[number, z][None] * padded_edge[z + dz].reshape(
+                        rhs // 8, 8, LANES
+                    )
+                    part = term if part is None else part + term
+                part = turn(part.reshape(rhs, LANES), -16 * dx)
+                total = part if total is None else total + part
+            result[dy] = total
+        return result
 
     def apply_operator(s):
         more = s + 1 < STEPS
         for z in range(nz):
-            near = sums(z, wide_edge, padded_edge, (-1, 0, 1) if more else (-1, 1))
-            here = sums(z, wide, padded, (-1, 0, 1))
+            near = edge_sums(z, (-1, 0, 1) if more else (-1, 1))
+            here = sums(z)
+            before, after = near[-1], near[1]
             for x in range(rows):
-                before, after = near[-1][x], near[1][x]
+                at = 16 * (x + 1)
                 value = here[0][x]
-                value = value + jnp.where(lane == 0, turn(before, -3), turn(here[-1][x], 1))
                 value = value + jnp.where(
-                    lane == LANES - 1, turn(after, LANES - 13), turn(here[1][x], -1)
+                    lane == 0, turn(before, -3 - at), turn(here[-1][x], 1)
+                )
+                value = value + jnp.where(
+                    lane == LANES - 1, turn(after, LANES - 13 - at), turn(here[1][x], -1)
                 )
                 if s > 0:
                     value = 2.0 * value - tile[s - 1, z, x]
                 keep(s + 1, z * rows + x, value)
                 if more:
                     tile[s + 1, z, x] = value
-                    value = near[0][x] + turn(before, 1) + turn(after, -1)
-                    if s > 0:
-                        value = 2.0 * value - edge[s - 1, z, x]
-                    edge[s + 1, z, x] = value
+            if more:
+                value = near[0] + turn(before, 1) + turn(after, -1)
+                if s > 0:
+                    value = 2.0 * value - edge[s - 1, z]
+                edge[s + 1, z] = value
 
     def fill_padded(s):
         for z in range(nz):
             for x in range(rows):
                 padded[z, 1 + x] = tile[s, z, x]
-                padded_edge[z, 1 + x] = edge[s, z, x]
 
     def group_rows(g):
         return pl.ds(GROUPS[g][0] * rhs, (GROUPS[g][1] - GROUPS[g][0]) * rhs)
@@ -408,9 +435,10 @@
     for number in range(27):
         weight = turn(weights_of(number), number % 3 - 1)
         wide[number] = jnp.broadcast_to(weight[:, None, :], (cells, 8, LANES))
-        own_c[number] = edge_own(weights_of(number), number % 3 - 1)
+        own_c[number] = edge_own(weights_of(number))
     for number in range(cells):
-        own_edge[number] = edge_own(tile[0, number // rows, number % rows])
+        z, x = number // rows, number % rows
+        own_edge[number] = edge_own(tile[0, z, x], 16 * (x + 1))
 
     last = BLOCKS - 1
     for s in range(STEPS):
@@ -435,14 +463,27 @@
                     coefficient_copy(side).wait_recv()
                     for slot in range(3):
                         column_copy(side, slot).wait_recv()
-            for number in range(cells):
-                z, x = number // rows, number % rows
-                edge[0, z, x] = edge_windows(own_edge[number], landed[0, 1], landed[1, 1], number)
+            for z in range(nz):
+                total = jnp.zeros((rhs, LANES), jnp.float32)
+                for x in range(rows):
+                    number, at = z * rows + x, 16 * (x + 1)
+                    total = total + edge_windows(
+                        own_edge[number], landed[0, 1], landed[1, 1], number, at
+                    )
+                edge[0, z] = total
+            place_x = lax.broadcasted_iota(jnp.int32, (cells, LANES), 0) % rows
             for number in range(27):
-                weight = edge_windows(
-                    own_c[number], landed_c[0], landed_c[1], number, number % 3 - 1
-                )
-                wide_edge[number] = jnp.broadcast_to(weight[:, None, :], (cells, 8, LANES))
+                dx, dy = number // 3 % 3 - 1, number % 3 - 1
+                weight = edge_windows(own_c[number], landed_c[0], landed_c[1], number)
+                spread = jnp.zeros((cells, LANES), jnp.float32)
+                for x in range(rows):
+                    moved = turn(weight, 16 * (x + 1 + dx) + dy)
+                    spread = jnp.where(place_x == x, moved, spread)
+                for z in range(nz):
+                    line = spread[z * rows : z * rows + 1]
+                    for x in range(1, rows):
+                        line = line + spread[z * rows + x : z * rows + x + 1]
+                    wide_edge[number, z] = jnp.broadcast_to(line, (8, LANES))
             fill_padded(s)
         put_ghosts(s)
         apply_operator(s)
@@ -528,9 +569,9 @@
             pltpu.VMEM((size, columns), f32),
             pltpu.VMEM((27 * cells, columns), f32),
             pltpu.VMEM((27, cells, 8, LANES), f32),
-            pltpu.VMEM((27, cells, 8, LANES), f32),
+            pltpu.VMEM((27, nz, 8, LANES), f32),
             pltpu.VMEM((STEPS, nz, rows, rhs, LANES), f32),
-            pltpu.VMEM((STEPS, nz, rows, rhs, LANES), f32),
+            pltpu.VMEM((STEPS, nz, rhs, LANES), f32),
             pltpu.VMEM((STEPS, 2, nz, rhs, LANES), f32),
             pltpu.VMEM((2, rhs, LANES), f32),
             pltpu.VMEM((2, 3, rhs, LANES), f32),
@@ -539,7 +580,7 @@
             pltpu.VMEM((STEPS, 2, 8, LANES), f32),
             pltpu.VMEM((STEPS, 2, 8, LANES), f32),
             pltpu.VMEM((nz, rows + 2, rhs, LANES), f32),
-            pltpu.VMEM((nz, rows + 2, rhs, LANES), f32),
+            pltpu.VMEM((nz, rhs, LANES), f32),
             pltpu.VMEM((cells, rhs, LANES), f32),
             pltpu.VMEM((27, cells, LANES), f32),
             pltpu.VMEM((2 * nx, total, LANES), f32),

time: 31.6 us -> 31.9 us (level)
  no operation moved by 1% of the time
where the time goes in v6:
time: 31.9 us; the launch traced here: 31.8 us
  Pallas kernels  31.1 us (97%)
  between operations  0.64 us (2%)
    pallas_call x1, Pallas kernels, local(): pl.pallas_call(functools.partial(kernel, nx, ny, rhs, nz, rows, nx * ny *...  28.9 us
    pallas_call x1, Pallas kernels, local(): pl.pallas_call(functools.partial(finish_kernel, rhs, cells), out_shape=(s...  2.28 us

profile of v6, /device:TPU:0, one launch (start us, length us, event | category | flops | bytes accessed | tf_op | source)
XLA Modules:
  0.0 31.8 jit_solution(12958025594280932597)
XLA Ops:
  0.6 28.9 %shard_map.41 = (bf16[80,2048]{1,0:T(8,128)(2,1)S(1)}, bf16[80,2048]{1,0:T(8,128)(2,1)S(1)}, f32[4,256,128]{2,1,0:T(8,128)S(1)}, f32[16,128]{1,0:T(8,128)S(1)}, ...) custom-call(f32[256,128]{1,0:T(8,128)} %bitcast.4, f32[432,128]{1,0:T(8,128)} %bitcast.3), custom_call_target="tpu_custom_call" | custom-call | tf_op jit(solution)/shard_map/pallas_call | solution.py:555
  29.5 2.3 %shard_map.42 = (f32[5,256,128]{2,1,0:T(8,128)}, f32[80,80]{1,0:T(8,128)}) custom-call(bf16[80,2048]{1,0:T(8,128)(2,1)S(1)} %get-tuple-element.11.high, bf16[80,2048]{1,0:T(8,128)(2,1)S(1)} %get-tuple-element.12.low, f32[4,256,128]{2,1,0:T(8,128)S(1)} %get-tuple-element.13.first, f32[16,128]{1,0:T(8,128)S(1)} %get-tuple-element.14.last_gram, ...), custom_call_target="tpu_custom_call" | custom-call | tf_op jit(solution)/shard_map/pallas_call | solution.py:605

commit v7 on v6

--- a/solution.py
+++ b/solution.py
@@ -14,7 +14,7 @@
 SIDES = (0, 1)
 NT = (((1,), (1,)), ((), ()))
 NN = (((1,), (0,)), ((), ()))
-GROUPS = ((0, 2), (2, 4), (4, 5))
+GROUPS = ((0, 1), (1, 3), (3, 4), (4, 5))
 
 
 def split(value):
@@ -442,14 +442,17 @@
 
     last = BLOCKS - 1
     for s in range(STEPS):
+        if s == 0:
+            local_gram(0)
         if s == 1:
-            local_gram(0)
+            gram_over_gx(0)
         if s == 2:
-            gram_over_gx(0)
-        if s == 3:
             local_gram(1)
             wait_gram(0)
             factor_block(0)
+        if s == 3:
+            local_gram(2)
+            gram_over_gx(1)
         if s > 0:
             fill_padded(s)
         for side in SIDES:
@@ -491,12 +494,15 @@
             send_rows(s + 1)
             send_edges(s + 1)
 
-    local_gram(2)
-    gram_over_gx(1)
+    local_gram(3)
+    gram_over_gx(2)
+    wait_gram(1)
     factor_block(1)
     apply_block(0)
+    gram_over_gx(3)
+    factor_block(2)
     apply_block(1)
-    gram_over_gx(2)
+    apply_block(2)
     for s in range(STEPS):
         for side in SIDES:
             row_copy(s, side).wait_send()
@@ -509,15 +515,14 @@
                 column_copy(side, slot).wait_send()
             coefficient_copy(side).wait_send()
     finish_gram(0)
-    wait_gram(1)
-    factor_block(2)
-    apply_block(2)
+    finish_gram(1)
+    wait_gram(2)
     factor_block(3)
     apply_block(3)
-    finish_gram(1)
-    wait_gram(2)
+    finish_gram(2)
+    wait_gram(3)
     last_gram[...] = gram_block(last)
-    finish_gram(2)
+    finish_gram(3)
 
 
 def finish_kernel(

time: 31.9 us -> 33.1 us (1.038)
  Pallas kernels: 31.1 us -> 32.3 us
    pallas_call x1, Pallas kernels: 28.9 us -> 30 us  [local(): pl.pallas_call(functools.partial(kernel, nx, ny, rhs, nz, rows, nx * ny *...]
where the time goes in v7:
time: 33.1 us; the launch traced here: 32.9 us
  Pallas kernels  32.3 us (98%)
  between operations  0.64 us (2%)
    pallas_call x1, Pallas kernels, local(): pl.pallas_call(functools.partial(kernel, nx, ny, rhs, nz, rows, nx * ny *...  30 us
    pallas_call x1, Pallas kernels, local(): pl.pallas_call(functools.partial(finish_kernel, rhs, cells), out_shape=(s...  2.28 us

profile of v7, /device:TPU:0, one launch (start us, length us, event | category | flops | bytes accessed | tf_op | source)
XLA Modules:
  0.0 32.9 jit_solution(7758150301797037559)
XLA Ops:
  0.6 30.0 %shard_map.41 = (bf16[80,2048]{1,0:T(8,128)(2,1)S(1)}, bf16[80,2048]{1,0:T(8,128)(2,1)S(1)}, f32[4,256,128]{2,1,0:T(8,128)S(1)}, f32[16,128]{1,0:T(8,128)S(1)}, ...) custom-call(f32[256,128]{1,0:T(8,128)} %bitcast.4, f32[432,128]{1,0:T(8,128)} %bitcast.3), custom_call_target="tpu_custom_call" | custom-call | tf_op jit(solution)/shard_map/pallas_call | solution.py:560
  30.6 2.3 %shard_map.42 = (f32[5,256,128]{2,1,0:T(8,128)}, f32[80,80]{1,0:T(8,128)}) custom-call(bf16[80,2048]{1,0:T(8,128)(2,1)S(1)} %get-tuple-element.11.high, bf16[80,2048]{1,0:T(8,128)(2,1)S(1)} %get-tuple-element.12.low, f32[4,256,128]{2,1,0:T(8,128)S(1)} %get-tuple-element.13.first, f32[16,128]{1,0:T(8,128)S(1)} %get-tuple-element.14.last_gram, ...), custom_call_target="tpu_custom_call" | custom-call | tf_op jit(solution)/shard_map/pallas_call | solution.py:610
